TPU v7x, 256 devices: a whole 4x4x8 slice. The times are simulated.
256 devices in a mesh: state: 8 (over z), basis: 32 (over x, y, core).
Axes of the slice: x: 4, y: 4, z: 8, core: 2. Of those that a mesh axis runs over, the one named last changes fastest.
Arguments:
- states: float32 [16, 64, 64000], P('state', 'basis'), may hold values from -40 to 40
- membrane_step: float32 [40, 40], replicated, may hold values from -1 to 1
- cavity_forward: float32 [64, 64], replicated, may hold values from -0.75 to 0.75
- coupling: float32 [64, 40], replicated, may hold values from 0.25 to 1
- membrane_forward: float32 [40, 40], replicated, may hold values from -1 to 1
- cavity_back: float32 [64, 64], replicated, may hold values from -9 to 9
- membrane_back: float32 [40, 40], replicated, may hold values from -1 to 1
Outputs:
- orthonormal: float32 [16, 64, 64000], P('state', 'basis')
All inputs are finite; a program needn't handle non-finite values.
Results may differ from a plain program's by a relative error of at most 0.000075.
Values sent between devices are 32-bit elements; how exact they have to be, the bound alone decides.
No kernel may reach another device: no remote copies, remote signals or barrier semaphores. Data moves between devices by JAX's collectives and lax.ppermute only.
A program may use at most 192 MiB of HBM per device.

v0:
```python
import functools

import jax
import jax.numpy as jnp
from jax import lax
from jax.sharding import Mesh
from jax.sharding import PartitionSpec as P

BASIS = ("basis_0", "basis_1", "basis_2")
STATE_BASIS = ("state", "basis_0", "basis_1", "basis_2")


def in_blocks(value, dim, size):
    before, after = (value.shape[:dim], value.shape[dim + 1 :])
    return jnp.moveaxis(value.reshape(*before, size, -1, *after), dim, 0)


def joined_along(pieces, dim):
    shape = list(pieces.shape[1:])
    shape[dim] *= pieces.shape[0]
    return jnp.moveaxis(pieces, 0, dim).reshape(shape)


def moved_by_axis(pieces, axes, turns):
    shape = [lax.axis_size(a) for a in axes]
    pieces = pieces.reshape(*shape, *pieces.shape[1:])
    for k in turns:
        pieces = lax.all_to_all(pieces, axes[k], split_axis=k, concat_axis=k, tiled=True)
    return pieces.reshape(-1, *pieces.shape[len(axes) :])


def exchange_by_chip(value, groups, turns, split_dim, concat_dim):
    size = lax.axis_size(groups[0]) * lax.axis_size(groups[1])
    pieces = in_blocks(value, split_dim, size)
    return joined_along(moved_by_axis(pieces, groups, turns), concat_dim)


def one_axis_at_a_time(value, axes):
    return functools.reduce(lax.psum, axes, value)


def one_exchange(value, axis, axes, splits, concats):
    sizes = [lax.axis_size(a) for a in axes]
    pieces = in_blocks(value, splits[0], sizes[0])
    pieces = jnp.moveaxis(in_blocks(pieces, splits[1] + 1, sizes[1]), 0, 1)
    inside = pieces.shape[2:]
    pieces = pieces.reshape(-1, *inside)
    pieces = lax.all_to_all(pieces, axis, split_axis=0, concat_axis=0, tiled=True)
    pieces = joined_along(pieces.reshape(*sizes, *inside), concats[0] + 1)
    return joined_along(pieces, concats[1])


def body(
    states, membrane_step, cavity_forward, coupling, membrane_forward, cavity_back, membrane_back
):
    highest = lax.Precision.HIGHEST
    panel_size, level_count, joint = states.shape
    levels_all = cavity_forward.shape[0]
    membrane_levels = membrane_step.shape[0]
    basis_total = float(levels_all * joint)
    head = jnp.einsum(
        "ab,scbr->scar",
        membrane_step,
        states.reshape(panel_size, level_count, membrane_levels, joint // membrane_levels),
        precision=highest,
    )
    head = head.reshape(panel_size, level_count, joint)
    panel_block = exchange_by_chip(head, (("basis_0", "basis_1"), "basis_2"), (1, 0), 2, 1)
    items, cavity_all, columns = panel_block.shape
    grid = jnp.einsum("qc,kcr->kqr", cavity_forward, panel_block, precision=highest)
    grid = jnp.einsum(
        "kqtm,nm->kqtn",
        grid.reshape(items, cavity_all, columns // membrane_levels, membrane_levels),
        membrane_forward,
        precision=highest,
    )
    weighted = grid * coupling[None, :, None, :]
    backward = jnp.einsum("kqtn,mn->kqtm", weighted, membrane_back, precision=highest)
    backward = backward.reshape(items, cavity_all, columns)
    stepped = jnp.einsum("cq,kqr->kcr", cavity_back, backward, precision=highest)
    spread = lax.all_to_all(stepped, "state", split_axis=2, concat_axis=0, tiled=True)
    state_total, spread_levels, spread_cols = spread.shape
    flattened = spread.reshape(state_total, -1)
    partial_gram = jnp.dot(flattened, flattened.T, precision=highest)
    gram = one_axis_at_a_time(partial_gram, STATE_BASIS) / basis_total
    lower_factor = jnp.linalg.cholesky(gram)
    identity = jnp.eye(state_total, dtype=gram.dtype)
    inverse = lax.linalg.triangular_solve(lower_factor, identity, left_side=True, lower=True)
    local_result = jnp.dot(inverse, flattened, precision=highest)
    local_result = local_result.reshape(state_total, spread_levels, spread_cols)
    return one_exchange(local_result, STATE_BASIS, ("state", BASIS), (0, 1), (2, 2))


def solution(mesh):
    split = Mesh(
        mesh.devices.reshape(mesh.shape["state"], 4, 4, 2),
        ("state", "basis_0", "basis_1", "basis_2"),
    )
    in_specs = (P("state", BASIS, None), P(), P(), P(), P(), P(), P())
    out_specs = P("state", BASIS, None)
    return jax.shard_map(body, mesh=split, in_specs=in_specs, out_specs=out_specs, check_vma=False)
```

profile of v0, /device:TPU:1, one launch (start us, length us, event | category | flops | bytes accessed | tf_op | source)
XLA Modules:
  0.0 178.6 jit_solution(9695296767113628193)
XLA Ops:
  0.0 1.9 %reshape.48 = f32[2,2,40,1600]{3,2,1,0:T(8,128)S(1)} reshape(f32[2,2,64000]{2,1,0:T(2,128)} %param.7) | data formatting | bytes 2048000 | tf_op jit(solution)/shard_map/reshape | solution.py:64
  5.1 7.4 %all_to_all.30 = f32[16,2,2,2,2000]{4,0,3,2,1:T(8,128)S(1)} all-to-all(f32[16,2,2,2,2000]{4,0,3,2,1:T(8,128)S(1)} %copy.47), channel_id=1, replica_groups=mesh['state'=8,'basis_0'=4,'basis_1'=4,'basis_2'=2] {'basis_2'}, dimensions={1} | all-to-all | bytes 2048000 | tf_op jit(solution)/shard_map/all_to_all | solution.py:28
  13.4 20.8 %all_to_all.31 = f32[16,2,2,2,2000]{4,1,3,2,0:T(2,128)S(1)} all-to-all(f32[16,2,2,2,2000]{4,1,3,2,0:T(2,128)S(1)} %copy.48), channel_id=1, replica_groups=mesh['state'=8,'basis_0'=4,'basis_1'=4,'basis_2'=2] {'basis_0','basis_1'}, dimensions={0} | all-to-all | bytes 2048000 | tf_op jit(solution)/shard_map/all_to_all | solution.py:28
  35.1 1.7 reshape.51
  36.8 2.3 %convolution_bitcast_fusion.2 = f32[2,64,2000]{2,1,0:T(8,128)S(1)} fusion(f32[2,64,2000]{2,1,0:T(8,128)} %reshape.51, f32[64,64]{1,0:T(8,128)S(1)} %copy-done), kind=kOutput, calls=%fused_computation.2 | convolution fusion | flops 196608000 | bytes 2064384 | tf_op jit(solution)/shard_map/qc,kcr->kqr/dot_general | solution.py:70
  39.8 1.9 %fusion.8 = f32[2,64,50,40]{1,3,2,0:T(8,128)S(1)} fusion(f32[2,64,50,40]{1,3,2,0:T(8,128)S(1)} %bitcast.84, f32[40,40]{1,0:T(8,128)S(1)} %copy-done.3), kind=kOutput, calls=%fused_computation.13 | convolution fusion | flops 122880000 | bytes 2054400 | tf_op jit(solution)/shard_map/kqtm,nm->kqtn/dot_general | solution.py:71
  41.7 1.9 %fusion = f32[2,64,50,40]{1,3,2,0:T(8,128)S(1)} fusion(f32[2,64,50,40]{1,3,2,0:T(8,128)S(1)} %fusion.8, f32[64,40]{0,1:T(8,128)S(1)} %copy-done.4, f32[40,40]{1,0:T(8,128)S(1)} %copy-done.5), kind=kOutput, calls=%fused_computation.3 | convolution fusion | flops 123136000 | bytes 2064640 | tf_op jit(solution)/shard_map/kqtn,mn->kqtm/dot_general | solution.py:78
  43.7 2.3 %convolution_bitcast_fusion.1 = f32[2,64,2000]{2,1,0:T(8,128)S(1)} fusion(f32[2,64,2000]{1,2,0:T(8,128)S(1)} %bitcast.85, f32[64,64]{1,0:T(8,128)S(1)} %copy-done.1), kind=kOutput, calls=%fused_computation.1 | convolution fusion | flops 196608000 | bytes 2064384 | tf_op jit(solution)/shard_map/cq,kqr->kcr/dot_general | solution.py:80
  46.0 1.9 %copy.53 = f32[2,64,2000]{1,0,2:T(2,128)S(1)} copy(f32[2,64,2000]{2,1,0:T(8,128)S(1)} %convolution_bitcast_fusion.1) | data formatting | bytes 2048000 | tf_op jit(solution)/shard_map/cq,kqr->kcr/transpose | solution.py:80
  47.9 2.1 %reshape.67 = f32[8,1,32000]{2,1,0:T(1,128)S(1)} reshape(f32[2000,2,64]{2,1,0:T(2,128)S(1)} %bitcast.86) | data formatting | bytes 2048000
  50.0 33.3 %all_to_all.32 = f32[8,1,32000]{2,1,0:T(1,128)S(1)} all-to-all(f32[8,1,32000]{2,1,0:T(1,128)S(1)} %reshape.67), channel_id=1, replica_groups=mesh['state'=8,'basis_0'=4,'basis_1'=4,'basis_2'=2] {'state'}, dimensions={0} | all-to-all | bytes 2048000 | tf_op jit(solution)/shard_map/all_to_all | solution.py:81
  83.8 3.1 %reduce.6 = f32[8,32000]{1,0:T(8,128)S(1)} reduce(f32[8,1,32000]{2,1,0:T(1,128)S(1)} %all_to_all.32, f32[]{:T(128)} %broadcast.49), dimensions={1}, to_apply=%all_to_all.22.reduce_sub_computation | reduce | bytes 2048004 | tf_op jit(solution)/shard_map/all_to_all | solution.py:81
  86.9 1.3 reshape.68
  89.8 1.4 fusion.16
  91.2 11.1 %psum.28 = f32[16,16]{0,1:T(8,128)S(1)} all-reduce(f32[16,16]{0,1:T(8,128)S(1)} %fusion.16), channel_id=1, replica_groups=mesh['state'=8,'basis_0'=4,'basis_1'=4,'basis_2'=2] {'state'}, use_global_device_ids=true, to_apply=%region_0.0 | all-reduce | flops 256 | bytes 2048 | tf_op jit(solution)/shard_map/psum | solution.py:39
  102.3 7.3 %psum.29 = f32[16,16]{0,1:T(8,128)S(1)} all-reduce(f32[16,16]{0,1:T(8,128)S(1)} %psum.28), channel_id=1, replica_groups=mesh['state'=8,'basis_0'=4,'basis_1'=4,'basis_2'=2] {'basis_0'}, use_global_device_ids=true, to_apply=%region_1.0 | all-reduce | flops 256 | bytes 2048 | tf_op jit(solution)/shard_map/psum | solution.py:39
  109.6 7.0 %psum.30 = f32[16,16]{0,1:T(8,128)S(1)} all-reduce(f32[16,16]{0,1:T(8,128)S(1)} %psum.29), channel_id=1, replica_groups=mesh['state'=8,'basis_0'=4,'basis_1'=4,'basis_2'=2] {'basis_1'}, use_global_device_ids=true, to_apply=%region_2.0 | all-reduce | flops 256 | bytes 2048 | tf_op jit(solution)/shard_map/psum | solution.py:39
  116.6 13.3 %psum.31 = f32[16,16]{0,1:T(8,128)S(1)} all-reduce(f32[16,16]{0,1:T(8,128)S(1)} %psum.30), channel_id=1, replica_groups=mesh['state'=8,'basis_0'=4,'basis_1'=4,'basis_2'=2] {'basis_2'}, use_global_device_ids=true, to_apply=%region_3.0 | all-reduce | flops 256 | bytes 2048 | tf_op jit(solution)/shard_map/psum | solution.py:39
  130.0 1.5 cholesky.17
  132.8 1.2 custom-call.6
  134.2 1.9 %dot_general.32 = f32[32,2,250,16]{2,1,0,3:T(2,128)S(1)} reshape(f32[16000,16]{0,1:T(8,128)S(1)} %bitcast.83) | data formatting | bytes 2048000 | tf_op jit(solution)/shard_map/dot_general | solution.py:89
  136.1 1.5 convolution_bitcast_fusion.3
  139.0 36.1 %all_to_all.33 = f32[256,2,2,250]{3,2,1,0:T(2,128)S(1)} all-to-all(f32[256,2,2,250]{3,2,1,0:T(2,128)S(1)} %copy.61), channel_id=1, replica_groups=mesh['state'=8,'basis_0'=4,'basis_1'=4,'basis_2'=2] {'state','basis_0','..., dimensions={0} | all-to-all | bytes 2048000 | tf_op jit(solution)/shard_map/all_to_all | solution.py:48
  176.5 2.2 %reshape.58 = f32[2,2,64000]{2,1,0:T(2,128)} reshape(f32[2,2,32,2000]{3,2,1,0:T(8,128)S(1)} %bitcast.93) | data formatting | bytes 2048000 | tf_op jit(solution)/shard_map/reshape | solution.py:21
  (36 shorter events, 12.0 us)
Async XLA Ops:
  0.0 36.8 %copy-start = (f32[64,64]{1,0:T(8,128)S(1)}, f32[64,64]{1,0:T(8,128)}, u32[]{:S(2)}) copy-start(f32[64,64]{1,0:T(8,128)} %param.9) | copy-start | bytes 49156
  0.0 1.9 %copy-start.2 = (f32[40,40]{1,0:T(8,128)S(1)}, f32[40,40]{1,0:T(8,128)}, u32[]{:S(2)}) copy-start(f32[40,40]{1,0:T(8,128)} %param.8) | copy-start | bytes 19204
  39.1 0.7 copy-start.3
  39.8 1.9 %copy-start.4 = (f32[64,40]{0,1:T(8,128)S(1)}, f32[64,40]{0,1:T(8,128)}, u32[]{:S(2)}) copy-start(f32[64,40]{0,1:T(8,128)} %param.10) | copy-start | bytes 30724
  39.8 1.9 %copy-start.5 = (f32[40,40]{1,0:T(8,128)S(1)}, f32[40,40]{1,0:T(8,128)}, u32[]{:S(2)}) copy-start(f32[40,40]{1,0:T(8,128)} %param.13) | copy-start | bytes 19204
  41.7 1.9 %copy-start.1 = (f32[64,64]{1,0:T(8,128)S(1)}, f32[64,64]{1,0:T(8,128)}, u32[]{:S(2)}) copy-start(f32[64,64]{1,0:T(8,128)} %param.12) | copy-start | bytes 49156
where the time goes:
time: 179 us
  blocking collectives  136 us (76%)
  local copies, waits for them, and re-layouts  22.6 us (13%)
  matrix products  12.4 us (7%)
  other arithmetic  7.09 us (4%)
    psum x4, blocking collectives, one_axis_at_a_time(): return functools.reduce(lax.psum, axes, value)  38.7 us
    all_to_all x1, blocking collectives, one_exchange(): lax.all_to_all(pieces, axis, split_axis=0, concat_axis=0, tiled=True)  36.1 us
    all_to_all x1, blocking collectives, body(): lax.all_to_all(stepped, 'state', split_axis=2, concat_axis=0, tiled=True)  33.3 us
    all_to_all x2, blocking collectives, moved_by_axis(): lax.all_to_all(pieces, axes[k], split_axis=k, concat_axis=k, tiled=True)  28.2 us
    reshape x3, local copies, waits for them, and re-layouts, joined_along(): return jnp.moveaxis(pieces, 0, dim).reshape(shape)  4.35 us
    unnamed x14, local copies, waits for them, and re-layouts  3.63 us

commit v1 on v0

v1 whole, which is shorter than its diff:
```python
import jax
import jax.numpy as jnp
from jax import lax
from jax.experimental import pallas as pl
from jax.experimental.pallas import tpu as pltpu
from jax.sharding import PartitionSpec as P

ROWS = 9
LANES = 128
F32 = jnp.float32
BF16 = jnp.bfloat16
HIGHEST = lax.Precision.HIGHEST
STATES = 16
LEVELS = 64
M = 40
WIDE = 3 * LANES
GROUP = 4
SMALL_VMEM = 24 << 20


def iota(shape, dim):
    return lax.broadcasted_iota(jnp.int32, shape, dim)


def exact_dot(a, b):
    return jnp.dot(a, b, precision=HIGHEST, preferred_element_type=F32)


def split(value):
    high = value.astype(BF16)
    return high, (value - high.astype(F32)).astype(BF16)


def dot3(a, b):
    (ah, al), (bh, bl) = a, b
    out = jnp.dot(ah, bl, preferred_element_type=F32) + jnp.dot(al, bh, preferred_element_type=F32)
    return out + jnp.dot(ah, bh, preferred_element_type=F32)


def head_kernel(states_ref, step_ref, send_ref, x_ref, extra_ref):
    row, col = iota((M, M), 0), iota((M, M), 1)
    order = (col == jnp.where(row < 20, 2 * row, 2 * row - 39)).astype(F32)
    row, col = iota((M, 48), 0), iota((M, 48), 1)
    even = (col < 20) & (row == 2 * col)
    odd = (col >= 24) & (col < 44) & (row == 2 * col - 47)
    step = exact_dot(exact_dot(order, step_ref[...]), (even | odd).astype(F32))

    x_ref[...] = jnp.zeros(x_ref.shape, F32)
    extra_ref[...] = jnp.zeros(extra_ref.shape, F32)
    send_ref[pl.ds(80 * ROWS + 8, 176, stride=ROWS), :] = jnp.zeros((176, LANES), F32)
    lane = iota((M, LANES), 1)
    lane20 = iota((20, LANES), 1)
    for s in range(2):
        for c in range(2):
            e = s * 2 + c

            def tile_in(u):
                return states_ref[pl.ds(s * 1000 + u * 2 + c, 20, stride=50), :]

            for v in range(13):
                x_ref[0:20, v * LANES : (v + 1) * LANES] = tile_in(v)
                low = pltpu.roll(tile_in(12 + v), 64, 1)
                high = pltpu.roll(tile_in(min(13 + v, 24)), 64, 1)
                x_ref[24:44, v * LANES : (v + 1) * LANES] = jnp.where(lane20 < 64, low, high)
            out = exact_dot(step, x_ref[...])
            tiles = [out[:, v * LANES : (v + 1) * LANES] for v in range(13)]

            def chunk(m):
                if m == 0:
                    return tiles[0]
                return jnp.where(
                    lane < 8 * m, pltpu.roll(tiles[m - 1], 8 * m, 1), pltpu.roll(tiles[m], 8 * m, 1)
                )

            last = chunk(12)
            tail = last[32:40]
            extras = [
                pltpu.roll(tiles[12], LANES - 24, 1),
                jnp.concatenate(
                    [
                        tail,
                        pltpu.roll(tail, LANES - 40, 1),
                        pltpu.roll(tail, LANES - 80, 1),
                        jnp.zeros((16, LANES), F32),
                    ],
                    axis=0,
                ),
            ]
            for m in range(12):
                g, h = m // 2, m % 2
                spare = pltpu.roll(extras[g], 120 - 8 * h, 1) if g < 2 else jnp.zeros((M, LANES), F32)
                block = jnp.where(lane < 120, chunk(m), spare)
                send_ref[pl.ds(g * M * ROWS + h * 4 + e, M, stride=ROWS), :] = block
            last = jnp.where(lane < 120, last, 0.0)
            for h in range(2):
                send_ref[pl.ds(240 * ROWS + h * 4 + e, 16, stride=ROWS), :] = last[16 * h : 16 * h + 16]
            inside = (lane >= 32 * e) & (lane < 32 * e + 24)
            for g in range(2):
                moved = pltpu.roll(extras[g], (32 * e - 16) % LANES, 1)
                extra_ref[g] += jnp.where(inside, moved, 0.0)
    for g in range(2):
        send_ref[pl.ds(g * M * ROWS + 8, M, stride=ROWS), :] = extra_ref[g]


def position(shape, dim):
    p = iota(shape, dim)
    h, lane = p >> 7, p & 127
    main = (h < 2) & (lane < 120)
    third = (lane >= 40).astype(jnp.int32) + (lane >= 80).astype(jnp.int32)
    slot = jnp.where(main, 3 * h + third, 6)
    level = jnp.where(main, lane - 40 * third, jnp.where(h < 2, 8 * h + lane - 120, 16 + lane))
    real = (h < 2) | (lane < 24)
    return jnp.where(real, slot, -1), jnp.where(real, level, -1)


def operands_kernel(
    forward_ref, coupling_ref, mem_forward_ref, back_ref, mem_back_ref, cf_ref, cb_ref, mf_ref, mb_ref, w_ref
):
    size = GROUP * LEVELS
    same = (iota((size, size), 0) >> 6) == (iota((size, size), 1) >> 6)
    tall = (iota((size, LEVELS), 1) == (iota((size, LEVELS), 0) & 63)).astype(F32)
    wide = (iota((LEVELS, size), 0) == (iota((LEVELS, size), 1) & 63)).astype(F32)

    def level_of(p):
        return 2 * (p & 31) + ((p >> 5) & 1)

    tall_level = (iota((size, LEVELS), 1) == level_of(iota((size, LEVELS), 0))).astype(F32)
    wide_level = (iota((LEVELS, size), 0) == level_of(iota((LEVELS, size), 1))).astype(F32)
    forward = exact_dot(tall, exact_dot(forward_ref[...], wide_level))
    back = exact_dot(tall_level, exact_dot(back_ref[...], wide))
    for ref, value in ((cf_ref, forward), (cb_ref, back)):
        ref[0], ref[1] = split(jnp.where(same, value, 0.0))

    slot_in, _ = position((WIDE, WIDE), 0)
    slot_out, _ = position((WIDE, WIDE), 1)
    same = (slot_in == slot_out) & (slot_in >= 0)
    _, level = position((WIDE, M), 0)
    down = (level == iota((WIDE, M), 1)).astype(F32)
    _, level = position((M, WIDE), 1)
    across = (level == iota((M, WIDE), 0)).astype(F32)
    for ref, matrix in ((mf_ref, mem_forward_ref), (mb_ref, mem_back_ref)):
        turned = lax.dot_general(
            down, matrix[...], (((1,), (1,)), ((), ())), precision=HIGHEST, preferred_element_type=F32
        )
        ref[0], ref[1] = split(jnp.where(same, exact_dot(turned, across), 0.0))
    w_ref[...] = exact_dot(coupling_ref[...], across)


def step_kernel(recv_ref, cf_ref, cb_ref, mf_ref, mb_ref, w_ref, main_ref, rest_ref, gram_ref, rows_ref):
    lane = iota((32, LANES), 1)
    cf, cb = (cf_ref[0], cf_ref[1]), (cb_ref[0], cb_ref[1])
    mf, mb = (mf_ref[0], mf_ref[1]), (mb_ref[0], mb_ref[1])
    w = jnp.concatenate([w_ref[...]] * GROUP, axis=0)
    size = GROUP * LEVELS
    for group in range(STATES // GROUP):
        parts = []
        for z in range(group * 2, group * 2 + 2):
            seventh = recv_ref[pl.ds(z * 32 * ROWS + 8, 32, stride=ROWS), :]
            for e in range(4):
                halves = [recv_ref[pl.ds(z * 32 * ROWS + h * 4 + e, 32, stride=ROWS), :] for h in range(2)]
                moved = pltpu.roll(seventh, LANES - 32 * e, 1) if e else seventh
                parts.append(jnp.concatenate(halves + [jnp.where(lane < 24, moved, 0.0)], axis=1))
        value = jnp.concatenate(parts, axis=0)
        value = dot3(cf, split(value))
        value = dot3(split(value), mf) * w
        value = dot3(split(value), mb)
        value = dot3(cb, split(value))
        for h in range(2):
            main_ref[h, group * size : (group + 1) * size, :] = value[:, h * LANES : (h + 1) * LANES]
        rest_ref[group * size : (group + 1) * size, :] = value[:, 2 * LANES :]

    for first in range(0, STATES, 4):
        for second in range(0, first + 4, 4):

            def add(tile, sums, first=first, second=second):
                start = pl.multiple_of(tile * 8, 8)
                for load in (
                    lambda st: main_ref[0, pl.ds(st * LEVELS + start, 8), :],
                    lambda st: main_ref[1, pl.ds(st * LEVELS + start, 8), :],
                    lambda st: rest_ref[pl.ds(st * LEVELS + start, 8), :],
                ):
                    a = [load(first + n) for n in range(4)]
                    b = a if first == second else [load(second + n) for n in range(4)]
                    sums = tuple(sums[p * 4 + q] + a[p] * b[q] for p in range(4) for q in range(4))
                return sums

            sums = lax.fori_loop(0, 8, add, (jnp.zeros((8, LANES), F32),) * 16)
            for p in range(4):
                for q in range(4):
                    total = jnp.sum(sums[p * 4 + q], axis=0, keepdims=True)
                    at = (first + p) * STATES + second + q
                    rows_ref[at : at + 1, :] = total
                    if first != second:
                        at = (second + q) * STATES + first + p
                        rows_ref[at : at + 1, :] = total
    flat = lax.dot_general(
        jnp.ones((32, LANES), F32), rows_ref[...], (((1,), (1,)), ((), ())), precision=HIGHEST,
        preferred_element_type=F32,
    )
    for h in range(2):
        gram_ref[pl.ds(h, 32, stride=2), :] = flat[:, h * LANES : (h + 1) * LANES]


def mix_kernel(scale, gram_ref, main_ref, rest_ref, send_ref, coef_ref):
    gram = gram_ref[0:2, :]
    for z in range(1, 8):
        gram = gram + gram_ref[2 * z : 2 * z + 2, :]
    gram = gram * scale
    flat = jnp.concatenate([gram[0:1], gram[1:2]], axis=1)
    row, col = iota((STATES, 2 * LANES), 0), iota((STATES, 2 * LANES), 1)
    spread = jnp.where((col >> 4) == row, flat, 0.0)
    row, col = iota((2 * LANES, LANES), 0), iota((2 * LANES, LANES), 1)
    square = exact_dot(spread, ((row & 15) == col).astype(F32))
    row, col = iota((STATES, LANES), 0), iota((STATES, LANES), 1)
    work = square + (col == row + STATES).astype(F32)
    for j in range(STATES - 1):
        pivot = work[j : j + 1, :]
        factor = work[:, j : j + 1] / work[j : j + 1, j : j + 1]
        work = work - jnp.where(row > j, factor, 0.0) * pivot
    diagonal = jnp.sum(jnp.where(col == row, work, 0.0), axis=1, keepdims=True)
    inverse = work / jnp.sqrt(diagonal)
    row, col = iota((STATES * STATES, STATES), 0), iota((STATES * STATES, STATES), 1)
    repeated = exact_dot(((row >> 4) == col).astype(F32), inverse)
    row, col = iota((STATES * STATES, LANES), 0), iota((STATES * STATES, LANES), 1)
    picked = jnp.where(col == (row & 15) + STATES, repeated, 0.0)
    coef_ref[...] = exact_dot(picked, jnp.ones((LANES, LANES), F32))

    lane = iota((8, LANES), 1)

    def mixed(loads):
        values = [[load(st) for load in loads] for st in range(STATES)]
        for t in range(STATES):
            sums = [None, None]
            for st in range(t + 1):
                factor = coef_ref[t * STATES + st : t * STATES + st + 1, :]
                for n in range(2):
                    term = factor * values[st][n]
                    sums[n] = term if sums[n] is None else sums[n] + term
            yield t, sums

    def tile(n, carry):
        start = pl.multiple_of(n * 8, 8)
        for c in range(2):
            loads = [
                lambda st, h=h: main_ref[h, pl.ds(st * LEVELS + c * 32 + start, 8), :] for h in range(2)
            ]
            for t, sums in mixed(loads):
                z, s = t // 2, t % 2
                for h in range(2):
                    at = (z * 32 + start) * ROWS + h * 4 + s * 2 + c
                    send_ref[pl.ds(at, 8, stride=ROWS), :] = sums[h]
        loads = [lambda st, c=c: rest_ref[pl.ds(st * LEVELS + c * 32 + start, 8), :] for c in range(2)]
        seventh = None
        for t, sums in mixed(loads):
            z, s = t // 2, t % 2
            for c in range(2):
                e = s * 2 + c
                value = pltpu.roll(sums[c], 32 * e, 1) if e else sums[c]
                seventh = value if e == 0 else seventh + value
            if s == 1:
                send_ref[pl.ds((z * 32 + start) * ROWS + 8, 8, stride=ROWS), :] = seventh
        return carry

    lax.fori_loop(0, 4, tile, 0)


def tail_kernel(recv_ref, out_ref, chunk_ref, tile_ref):
    lane = iota((M, LANES), 1)
    lane8 = iota((8, LANES), 1)
    lane20 = iota((20, LANES), 1)
    for s in range(2):
        for c in range(2):
            e = s * 2 + c
            for m in range(12):
                g, h = m // 2, m % 2
                chunk_ref[m] = recv_ref[pl.ds(g * M * ROWS + h * 4 + e, M, stride=ROWS), :]
            for h in range(2):
                chunk_ref[12, 16 * h : 16 * h + 16] = recv_ref[pl.ds(240 * ROWS + h * 4 + e, 16, stride=ROWS), :]
            extras = []
            for g in range(2):
                seventh = recv_ref[pl.ds(g * M * ROWS + 8, M, stride=ROWS), :]
                extra = jnp.where(
                    lane < 8, pltpu.roll(chunk_ref[2 * g], 8, 1), pltpu.roll(chunk_ref[2 * g + 1], 16, 1)
                )
                extras.append(jnp.where(lane < 16, extra, pltpu.roll(seventh, (16 - 32 * e) % LANES, 1)))
            first, second, third = (extras[1][8 * n : 8 * n + 8] for n in range(3))
            chunk_ref[12, 32:40] = jnp.where(
                lane8 < 40,
                first,
                jnp.where(lane8 < 80, pltpu.roll(second, 40, 1), pltpu.roll(third, 80, 1)),
            )
            chunk_ref[13] = extras[0]
            for v in range(13):
                low = pltpu.roll(chunk_ref[v], (LANES - 8 * v) % LANES, 1) if v else chunk_ref[v]
                high = pltpu.roll(chunk_ref[v + 1], 120 - 8 * v, 1)
                tile_ref[v] = jnp.where(lane < 120 - 8 * v, low, high)
            for u in range(25):
                if u < 12:
                    value = tile_ref[u, 0:20]
                else:
                    low = tile_ref[12, 0:20] if u == 12 else pltpu.roll(tile_ref[u - 13, 20:40], 64, 1)
                    high = pltpu.roll(tile_ref[u - 12, 20:40], 64, 1)
                    value = jnp.where(lane20 < 64, low, high)
                out_ref[pl.ds(s * 1000 + u * 2 + c, 20, stride=50), :] = value


def call(kernel, outs, scratch, cost):
    return pl.pallas_call(
        kernel,
        out_shape=outs,
        scratch_shapes=scratch,
        compiler_params=pltpu.CompilerParams(vmem_limit_bytes=SMALL_VMEM),
        cost_estimate=pl.CostEstimate(flops=cost, bytes_accessed=1 << 20, transcendentals=0),
    )


def shape(*dims, dtype=F32):
    return jax.ShapeDtypeStruct(dims, dtype)


def exchange(blocks, axes):
    count = 1
    for a in axes:
        count *= lax.axis_size(a)
    rows = blocks.shape[0] // count
    value = blocks.reshape(count, 1, rows * LANES)
    value = lax.all_to_all(value, axes, split_axis=0, concat_axis=0, tiled=True)
    return value.reshape(blocks.shape)


def body(states, membrane_step, cavity_forward, coupling, membrane_forward, cavity_back, membrane_back):
    panel, levels, joint = states.shape
    everyone = ("state", "basis")
    linear = states.reshape(panel, levels, joint // LANES, LANES)
    linear = jnp.swapaxes(linear, 1, 2).reshape(-1, LANES)
    blocks = shape(256 * ROWS, LANES)
    send = call(
        head_kernel,
        blocks,
        [pltpu.VMEM((48, 13 * LANES), F32), pltpu.VMEM((2, M, LANES), F32)],
        1 << 20,
    )(linear, membrane_step)
    size = GROUP * LEVELS
    cf, cb, mf, mb, w = call(
        operands_kernel,
        (
            shape(2, size, size, dtype=BF16),
            shape(2, size, size, dtype=BF16),
            shape(2, WIDE, WIDE, dtype=BF16),
            shape(2, WIDE, WIDE, dtype=BF16),
            shape(LEVELS, WIDE),
        ),
        [],
        1 << 27,
    )(cavity_forward, coupling, membrane_forward, cavity_back, membrane_back)
    recv = exchange(send, everyone)
    main, rest, gram = call(
        step_kernel,
        (shape(2, STATES * LEVELS, LANES), shape(STATES * LEVELS, LANES), shape(64, LANES)),
        [pltpu.VMEM((STATES * STATES, LANES), F32)],
        1 << 30,
    )(recv, cf, cb, mf, mb, w)
    gram = lax.all_to_all(gram.reshape(32, 2, LANES), "basis", split_axis=0, concat_axis=0, tiled=True)
    gram = jnp.broadcast_to(jnp.sum(gram, axis=0, keepdims=True), (8, 2, LANES))
    gram = lax.all_to_all(gram, "state", split_axis=0, concat_axis=0, tiled=True)
    scale = 1.0 / float(LEVELS * joint)
    send = call(
        lambda *refs: mix_kernel(scale, *refs), blocks, [pltpu.VMEM((STATES * STATES, LANES), F32)], 1 << 27
    )(gram.reshape(16, LANES), main, rest)
    recv = exchange(send, everyone)
    out = call(
        tail_kernel,
        shape(2000, LANES),
        [pltpu.VMEM((14, M, LANES), F32), pltpu.VMEM((13, M, LANES), F32)],
        1 << 20,
    )(recv)
    out = out.reshape(panel, joint // LANES, levels, LANES)
    return jnp.swapaxes(out, 1, 2).reshape(panel, levels, joint)


def solution(mesh):
    in_specs = (P("state", "basis", None), P(), P(), P(), P(), P(), P())
    out_specs = P("state", "basis", None)
    return jax.shard_map(body, mesh=mesh, in_specs=in_specs, out_specs=out_specs, check_vma=False)
```

time: 179 us -> 134 us (0.75)
  blocking collectives: 136 us -> 61.5 us
  waiting for transfers between devices: 0 us -> 28.4 us
  Pallas kernels: 0 us -> 18 us
  starting transfers between devices: 0 us -> 15.7 us
  local copies, waits for them, and re-layouts: 22.6 us -> 9.38 us
  matrix products: 12.4 us -> 0 us
  other arithmetic: 7.09 us -> 0.04 us
    psum x4 -> x0, blocking collectives: 38.7 us -> none  [one_axis_at_a_time(): return functools.reduce(lax.psum, axes, value)]
    all_to_all x4 -> x3, blocking collectives: 97.7 us -> 61.5 us  [the longest x1 39.7 us: exchange(): value = lax.all_to_all(value, axes, split_axis=0, concat_axis=0, tiled=True)]
    all_to_all x0 -> x1, waiting for transfers between devices: none -> 28.4 us  [exchange(): value = lax.all_to_all(value, axes, split_axis=0, concat_axis=0, tiled=True)]
    pallas_call x0 -> x5, Pallas kernels: none -> 18 us  [the longest x1 8.18 us: body(): call(step_kernel, (shape(2, STATES * LEVELS, LANES), shape(STATES * LEVEL...]
    all_to_all x0 -> x1, starting transfers between devices: none -> 15.7 us  [exchange(): value = lax.all_to_all(value, axes, split_axis=0, concat_axis=0, tiled=True)]
    dot_general x7 -> x0, matrix products: 12.2 us -> none  [the longest x1 2.29 us: body(): jnp.einsum('cq,kqr->kcr', cavity_back, backward, precision=highest)]
    reshape x7 -> x3, local copies, waits for them, and re-layouts: 8.3 us -> 3.4 us  [the longest x1 1.88 us: body(): linear = states.reshape(panel, levels, joint // LANES, LANES)]
    another operation x5 -> x0, other arithmetic: 4.01 us -> none  [the longest x3 2.13 us: body(): lower_factor = jnp.linalg.cholesky(gram)]
  transfers between devices with their start and end apart: 0 -> 1, of which waited for: 0 -> 1; matrix products, arithmetic and copies ran while one was open for 0% -> 0% of each run, Pallas kernels for 0% -> 2%
where the time goes in v1:
time: 134 us; the launch traced here: 133 us
  blocking collectives  61.5 us (46%)
  waiting for transfers between devices  28.4 us (21%)
  Pallas kernels  18 us (13%)
  starting transfers between devices  15.7 us (12%)
  local copies, waits for them, and re-layouts  9.38 us (7%)
    all_to_all x1, blocking collectives, exchange(): value = lax.all_to_all(value, axes, split_axis=0, concat_axis=0, tiled=True)  39.7 us
    all_to_all x1, waiting for transfers between devices, exchange(): value = lax.all_to_all(value, axes, split_axis=0, concat_axis=0, tiled=True)  28.4 us
    all_to_all x1, starting transfers between devices, exchange(): value = lax.all_to_all(value, axes, split_axis=0, concat_axis=0, tiled=True)  15.7 us
    all_to_all x1, blocking collectives, body(): lax.all_to_all(gram.reshape(32, 2, LANES), 'basis', split_axis=0, concat_...  12.9 us
    all_to_all x1, blocking collectives, body(): lax.all_to_all(gram, 'state', split_axis=0, concat_axis=0, tiled=True)  8.93 us
    pallas_call x1, Pallas kernels, body(): call(step_kernel, (shape(2, STATES * LEVELS, LANES), shape(STATES * LEVEL...  8.18 us
    unnamed x25, local copies, waits for them, and re-layouts  5.45 us
    pallas_call x1, Pallas kernels, body(): call(lambda *refs: mix_kernel(scale, *refs), blocks, [pltpu.VMEM((STATES...  3.18 us
  transfers between devices with their start and end apart: 1, of which 1 were waited for; matrix products, arithmetic and copies ran while one was open for 0% of the time, Pallas kernels for 2%

profile of v1, /device:TPU:1, one launch (start us, length us, event | category | flops | bytes accessed | tf_op | source)
XLA Modules:
  0.0 133.1 jit_solution(2392609992785062852)
XLA Ops:
  0.0 1.9 %reshape.31 = f32[2,2,500,128]{3,2,1,0:T(8,128)S(1)} reshape(f32[2,2,64000]{2,1,0:T(2,128)} %param.7) | data formatting | bytes 2048000 | tf_op jit(solution)/shard_map/reshape | solution.py:334
  1.9 0.0 copy-start
  1.9 0.5 copy.14
  2.4 0.2 copy-done
  2.6 2.7 %shard_map.73 = f32[2304,128]{1,0:T(8,128)} custom-call(f32[2000,128]{1,0:T(8,128)S(1)} %bitcast.14, f32[40,40]{1,0:T(8,128)S(1)} %copy-done), custom_call_target="tpu_custom_call" | custom-call | flops 1048576 | bytes 1048576 | tf_op jit(solution)/shard_map/pallas_call | solution.py:337
  5.4 15.7 %all-to-all-start = ((f32[256,1,1152]{2,1,0:T(1,128)}), f32[256,1,1152]{2,1,0:T(1,128)S(1)}, u32[]{:S(2)}, u32[]{:S(2)}) async-start(f32[256,1,1152]{2,1,0:T(1,128)} %bitcast.2), calls=%async_computation | async-start | bytes 2359296 | tf_op jit(solution)/shard_map/all_to_all | solution.py:327
  21.1 0.1 copy.16.coupling_ref
  21.2 2.5 %shard_map.74 = (bf16[2,256,256]{2,1,0:T(8,128)(2,1)S(1)}, bf16[2,256,256]{2,1,0:T(8,128)(2,1)S(1)}, bf16[2,384,384]{2,1,0:T(8,128)(2,1)S(1)}, bf16[2,384,384]{2,1,0:T(8,128)(2,1)S(1)}, f32[64,384]{1,0:T(8,128)S(1)}) custom-call(f32[64,64]{1,0:T(8,128)S(1)} %copy-done.1, f32[64,40]{1,0:T(8,128)S(1)} %copy.16.coupling_ref, f32[40,40]{1,0:T(8,128)S(1)} %copy-done.3, ...), custom_call_target="tpu_custom_call" | custom-call | flops 134217728 | bytes 1048576 | tf_op jit(solution)/shard_map/pallas_call | solution.py:344
  23.7 0.0 copy-start.5
  23.7 0.8 copy-done.5
  24.5 0.7 copy-done.7
  25.2 0.7 copy-done.9
  25.9 28.4 %all-to-all-done = f32[256,1,1152]{2,1,0:T(1,128)S(1)} async-done(((f32[256,1,1152]{2,1,0:T(1,128)}), f32[256,1,1152]{2,1,0:T(1,128)S(1)}, u32[]{:S(2)}, u32[]{:S(2)}) %all-to-all-start) | async-done | bytes 1179680 | tf_op jit(solution)/shard_map/all_to_all | solution.py:327
  54.3 1.1 copy-done.6
  55.4 0.9 copy-done.8
  56.3 0.9 copy-done.10
  57.3 8.2 %shard_map.75 = (f32[2,1024,128]{2,1,0:T(8,128)S(1)}, f32[1024,128]{1,0:T(8,128)S(1)}, f32[64,128]{1,0:T(8,128)S(1)}) custom-call(f32[2304,128]{1,0:T(8,128)S(1)} %bitcast.16, bf16[2,256,256]{2,1,0:T(8,128)(2,1)S(1)} %copy-done.8, bf16[2,256,256]{2,1,0:T(8,128)(2,1)S(1)} %copy-done.10, bf16[2,384,384]{2,1,0:T(8,128)(2,1)S(1)} %get-tuple-element.15.mf_ref, ...), custom_call_target="tpu_custom_call" | custom-call | flops 1073741824 | bytes 1048576 | tf_op jit(solution)/shard_map/pallas_call | solution.py:357
  65.5 12.9 %all_to_all.20 = f32[32,2,128]{2,1,0:T(2,128)S(1)} all-to-all(f32[32,2,128]{2,1,0:T(2,128)S(1)} %bitcast.18), channel_id=1, replica_groups=mesh['state'=8,'basis'=32] {'basis'}, dimensions={0} | all-to-all | bytes 65536 | tf_op jit(solution)/shard_map/all_to_all | solution.py:363
  78.4 8.9 %all_to_all.21 = f32[8,2,128]{2,1,0:T(2,128)S(1)} all-to-all(f32[8,2,128]{2,1,0:T(2,128)S(1)} %broadcast_in_dim.2), channel_id=1, replica_groups=mesh['state'=8,'basis'=32] {'state'}, dimensions={0} | all-to-all | bytes 16384 | tf_op jit(solution)/shard_map/all_to_all | solution.py:365
  87.3 3.2 %shard_map.76 = f32[2304,128]{1,0:T(8,128)S(1)} custom-call(f32[16,128]{1,0:T(8,128)S(1)} %bitcast.17, f32[2,1024,128]{2,1,0:T(8,128)S(1)} %get-tuple-element.19.refs_1_, f32[1024,128]{1,0:T(8,128)S(1)} %get-tuple-element.20.refs_2_), custom_call_target="tpu_custom_call" | custom-call | flops 134217728 | bytes 1048576 | tf_op jit(solution)/shard_map/pallas_call | solution.py:367
  90.5 39.7 %all_to_all.22 = f32[256,1,1152]{2,1,0:T(1,128)S(1)} all-to-all(f32[256,1,1152]{2,1,0:T(1,128)S(1)} %bitcast.13), channel_id=1, replica_groups=mesh['state'=8,'basis'=32] {'state','basis'}, dimensions={0} | all-to-all | bytes 2359296 | tf_op jit(solution)/shard_map/all_to_all | solution.py:327
  130.2 1.3 %shard_map.77 = f32[2000,128]{1,0:T(8,128)S(1)} custom-call(f32[2304,128]{1,0:T(8,128)S(1)} %bitcast.12), custom_call_target="tpu_custom_call" | custom-call | flops 1048576 | bytes 1048576 | tf_op jit(solution)/shard_map/pallas_call | solution.py:371
  131.6 0.1 copy.20
  131.7 1.4 %reshape.40 = f32[2,2,64000]{2,1,0:T(2,128)} reshape(f32[2,2,500,128]{3,2,1,0:T(8,128)S(1)} %bitcast.19) | data formatting | bytes 2048000 | tf_op jit(solution)/shard_map/reshape | solution.py:378
  (17 shorter events, 0.1 us)
Async XLA Ops:
  1.9 0.7 copy-start
  5.4 15.7 %copy-start.11 = (f32[64,40]{0,1:T(8,128)S(1)}, f32[64,40]{0,1:T(8,128)}, u32[]{:S(2)}) copy-start(f32[64,40]{0,1:T(8,128)} %param.10) | copy-start | bytes 30724
  5.4 15.8 %copy-start.1 = (f32[64,64]{1,0:T(8,128)S(1)}, f32[64,64]{1,0:T(8,128)}, u32[]{:S(2)}) copy-start(f32[64,64]{1,0:T(8,128)} %forward_ref.1) | copy-start | bytes 49156
  5.4 15.8 %copy-start.2 = (f32[64,64]{1,0:T(8,128)S(1)}, f32[64,64]{1,0:T(8,128)}, u32[]{:S(2)}) copy-start(f32[64,64]{1,0:T(8,128)} %back_ref.1) | copy-start | bytes 49156
  5.4 15.8 %copy-start.3 = (f32[40,40]{1,0:T(8,128)S(1)}, f32[40,40]{1,0:T(8,128)}, u32[]{:S(2)}) copy-start(f32[40,40]{1,0:T(8,128)} %mem_forward_ref.1) | copy-start | bytes 19204
  5.4 15.8 %copy-start.4 = (f32[40,40]{1,0:T(8,128)S(1)}, f32[40,40]{1,0:T(8,128)}, u32[]{:S(2)}) copy-start(f32[40,40]{1,0:T(8,128)} %mem_back_ref.1) | copy-start | bytes 19204
  5.4 48.9 %all-to-all-start = ((f32[256,1,1152]{2,1,0:T(1,128)}), f32[256,1,1152]{2,1,0:T(1,128)S(1)}, u32[]{:S(2)}, u32[]{:S(2)}) async-start(f32[256,1,1152]{2,1,0:T(1,128)} %bitcast.2), calls=%async_computation | async-start | bytes 2359296 | tf_op jit(solution)/shard_map/all_to_all | solution.py:327
  23.7 0.8 copy-start.5
  24.5 0.7 copy-start.7
  25.2 0.7 copy-start.9
  54.3 1.1 copy-start.6
  55.4 0.9 copy-start.8
  56.3 0.9 copy-start.10

commit v2 on v1

--- a/solution.py
+++ b/solution.py
@@ -1,6 +1,7 @@
 import jax
 import jax.numpy as jnp
 from jax import lax
+from jax.experimental.layout import Layout, with_layout_constraint
 from jax.experimental import pallas as pl
 from jax.experimental.pallas import tpu as pltpu
 from jax.sharding import PartitionSpec as P
@@ -13,9 +14,9 @@
 STATES = 16
 LEVELS = 64
 M = 40
-WIDE = 3 * LANES
 GROUP = 4
 SMALL_VMEM = 24 << 20
+LARGE_VMEM = 60 << 20
 
 
 def iota(shape, dim):
@@ -37,20 +38,28 @@
     return out + jnp.dot(ah, bh, preferred_element_type=F32)
 
 
-def head_kernel(states_ref, step_ref, send_ref, x_ref, extra_ref):
+def head_kernel(states_hbm, step_hbm, send_ref, states_ref, step_ref, x_ref, extra_ref, sems):
+    step_copy = pltpu.make_async_copy(step_hbm, step_ref, sems.at[2])
+    step_copy.start()
+    copies = []
+    for s in range(2):
+        part = pl.ds(s * 1000, 1000)
+        copies.append(pltpu.make_async_copy(states_hbm.at[part], states_ref.at[part], sems.at[s]))
+        copies[-1].start()
+    x_ref[...] = jnp.zeros(x_ref.shape, F32)
+    extra_ref[...] = jnp.zeros(extra_ref.shape, F32)
+    send_ref[pl.ds(80 * ROWS + 8, 176, stride=ROWS), :] = jnp.zeros((176, LANES), F32)
     row, col = iota((M, M), 0), iota((M, M), 1)
     order = (col == jnp.where(row < 20, 2 * row, 2 * row - 39)).astype(F32)
     row, col = iota((M, 48), 0), iota((M, 48), 1)
     even = (col < 20) & (row == 2 * col)
     odd = (col >= 24) & (col < 44) & (row == 2 * col - 47)
+    step_copy.wait()
     step = exact_dot(exact_dot(order, step_ref[...]), (even | odd).astype(F32))
-
-    x_ref[...] = jnp.zeros(x_ref.shape, F32)
-    extra_ref[...] = jnp.zeros(extra_ref.shape, F32)
-    send_ref[pl.ds(80 * ROWS + 8, 176, stride=ROWS), :] = jnp.zeros((176, LANES), F32)
     lane = iota((M, LANES), 1)
     lane20 = iota((20, LANES), 1)
     for s in range(2):
+        copies[s].wait()
         for c in range(2):
             e = s * 2 + c
 
@@ -102,21 +111,11 @@
         send_ref[pl.ds(g * M * ROWS + 8, M, stride=ROWS), :] = extra_ref[g]
 
 
-def position(shape, dim):
-    p = iota(shape, dim)
-    h, lane = p >> 7, p & 127
-    main = (h < 2) & (lane < 120)
-    third = (lane >= 40).astype(jnp.int32) + (lane >= 80).astype(jnp.int32)
-    slot = jnp.where(main, 3 * h + third, 6)
-    level = jnp.where(main, lane - 40 * third, jnp.where(h < 2, 8 * h + lane - 120, 16 + lane))
-    real = (h < 2) | (lane < 24)
-    return jnp.where(real, slot, -1), jnp.where(real, level, -1)
-
-
 def operands_kernel(
-    forward_ref, coupling_ref, mem_forward_ref, back_ref, mem_back_ref, cf_ref, cb_ref, mf_ref, mb_ref, w_ref
+    forward_ref, coupling_ref, mem_forward_ref, back_ref, mem_back_ref,
+    cf_ref, cb_ref, mf_ref, mb_ref, ef_ref, eb_ref, w_ref,
 ):
-    size = GROUP * LEVELS
+    size = 2 * LEVELS
     same = (iota((size, size), 0) >> 6) == (iota((size, size), 1) >> 6)
     tall = (iota((size, LEVELS), 1) == (iota((size, LEVELS), 0) & 63)).astype(F32)
     wide = (iota((LEVELS, size), 0) == (iota((LEVELS, size), 1) & 63)).astype(F32)
@@ -131,43 +130,98 @@
     for ref, value in ((cf_ref, forward), (cb_ref, back)):
         ref[0], ref[1] = split(jnp.where(same, value, 0.0))
 
-    slot_in, _ = position((WIDE, WIDE), 0)
-    slot_out, _ = position((WIDE, WIDE), 1)
-    same = (slot_in == slot_out) & (slot_in >= 0)
-    _, level = position((WIDE, M), 0)
-    down = (level == iota((WIDE, M), 1)).astype(F32)
-    _, level = position((M, WIDE), 1)
-    across = (level == iota((M, WIDE), 0)).astype(F32)
-    for ref, matrix in ((mf_ref, mem_forward_ref), (mb_ref, mem_back_ref)):
-        turned = lax.dot_general(
-            down, matrix[...], (((1,), (1,)), ((), ())), precision=HIGHEST, preferred_element_type=F32
-        )
-        ref[0], ref[1] = split(jnp.where(same, exact_dot(turned, across), 0.0))
-    w_ref[...] = exact_dot(coupling_ref[...], across)
-
-
-def step_kernel(recv_ref, cf_ref, cb_ref, mf_ref, mb_ref, w_ref, main_ref, rest_ref, gram_ref, rows_ref):
+    def threes(lane):
+        third = (lane >= 40).astype(jnp.int32) + (lane >= 80).astype(jnp.int32)
+        return jnp.where(lane < 120, third, -1), jnp.where(lane < 120, lane - 40 * third, -1)
+
+    def sevenths(lane):
+        real = (lane & 63) < 40
+        return jnp.where(real, lane >> 6, -1), jnp.where(real, lane & 63, -1)
+
+    for n, (place, fref, bref) in enumerate(((threes, mf_ref, mb_ref), (sevenths, ef_ref, eb_ref))):
+        slot_in, _ = place(iota((LANES, LANES), 0))
+        slot_out, _ = place(iota((LANES, LANES), 1))
+        same = (slot_in == slot_out) & (slot_in >= 0)
+        down = (place(iota((LANES, M), 0))[1] == iota((LANES, M), 1)).astype(F32)
+        across = (place(iota((M, LANES), 1))[1] == iota((M, LANES), 0)).astype(F32)
+        for ref, matrix in ((fref, mem_forward_ref), (bref, mem_back_ref)):
+            turned = lax.dot_general(
+                down, matrix[...], (((1,), (1,)), ((), ())), precision=HIGHEST, preferred_element_type=F32
+            )
+            ref[0], ref[1] = split(jnp.where(same, exact_dot(turned, across), 0.0))
+        w_ref[n] = exact_dot(coupling_ref[...], across)
+
+
+def twice(block):
+    zero = jnp.zeros_like(block)
+    return jnp.concatenate(
+        [jnp.concatenate([block, zero], axis=1), jnp.concatenate([zero, block], axis=1)], axis=0
+    )
+
+
+def turn(value, shift):
+    shift = shift % LANES
+    return pltpu.roll(value, shift, 1) if shift else value
+
+
+def step_kernel(
+    recv_ref, cf_ref, cb_ref, mf_ref, mb_ref, ef_ref, eb_ref, w_ref, main_ref, rest_ref, gram_ref, rows_ref
+):
+    cf, cb, mf, mb = ((twice(ref[0]), twice(ref[1])) for ref in (cf_ref, cb_ref, mf_ref, mb_ref))
+    ef, eb = (ef_ref[0], ef_ref[1]), (eb_ref[0], eb_ref[1])
+    w_half = jnp.concatenate([w_ref[0]] * GROUP, axis=0)
+    w_main = jnp.concatenate([w_half, w_half], axis=1)
+    w_rest = jnp.concatenate([w_ref[1]] * GROUP, axis=0)
+    size = GROUP * LEVELS
+    groups = STATES // GROUP
+
     lane = iota((32, LANES), 1)
-    cf, cb = (cf_ref[0], cf_ref[1]), (cb_ref[0], cb_ref[1])
-    mf, mb = (mf_ref[0], mf_ref[1]), (mb_ref[0], mb_ref[1])
-    w = jnp.concatenate([w_ref[...]] * GROUP, axis=0)
-    size = GROUP * LEVELS
-    for group in range(STATES // GROUP):
-        parts = []
-        for z in range(group * 2, group * 2 + 2):
-            seventh = recv_ref[pl.ds(z * 32 * ROWS + 8, 32, stride=ROWS), :]
-            for e in range(4):
-                halves = [recv_ref[pl.ds(z * 32 * ROWS + h * 4 + e, 32, stride=ROWS), :] for h in range(2)]
-                moved = pltpu.roll(seventh, LANES - 32 * e, 1) if e else seventh
-                parts.append(jnp.concatenate(halves + [jnp.where(lane < 24, moved, 0.0)], axis=1))
-        value = jnp.concatenate(parts, axis=0)
-        value = dot3(cf, split(value))
-        value = dot3(split(value), mf) * w
-        value = dot3(split(value), mb)
-        value = dot3(cb, split(value))
-        for h in range(2):
-            main_ref[h, group * size : (group + 1) * size, :] = value[:, h * LANES : (h + 1) * LANES]
-        rest_ref[group * size : (group + 1) * size, :] = value[:, 2 * LANES :]
+    parts = []
+    for part in range(2):
+        sevenths = [recv_ref[pl.ds((2 * g + part) * 32 * ROWS + 8, 32, stride=ROWS), :] for g in range(groups)]
+        for e in range(4):
+            value = turn(sevenths[3], 32 * (3 - e))
+            for g in range(2, -1, -1):
+                value = jnp.where(lane < 32 * g + 32, turn(sevenths[g], 32 * (g - e)), value)
+            parts.append(jnp.where((lane & 31) < 24, value, 0.0))
+    rest = dot3(cf, split(jnp.concatenate(parts, axis=0)))
+
+    lane = iota((size, LANES), 1)
+    rest_back = jnp.zeros((size, LANES), F32)
+    for pair in range(groups // 2):
+        mains = []
+        extra = jnp.zeros((size, LANES), F32)
+        for half in range(2):
+            group = 2 * pair + half
+            parts = []
+            for z in range(group * 2, group * 2 + 2):
+                for e in range(4):
+                    tiles = [recv_ref[pl.ds(z * 32 * ROWS + h * 4 + e, 32, stride=ROWS), :] for h in range(2)]
+                    parts.append(jnp.concatenate(tiles, axis=1))
+            value = dot3(cf, split(jnp.concatenate(parts, axis=0)))
+            at = 64 * half
+            moved = jnp.where(lane < at + 16, turn(value[:, LANES:], at + 16), turn(rest, at + 16 - 32 * group))
+            moved = jnp.where(lane < at + 8, turn(value[:, :LANES], at + 8), moved)
+            extra = jnp.where((lane >= at) & (lane < at + 40), moved, extra)
+            value = dot3(split(value), mf) * w_main
+            mains.append(dot3(split(value), mb))
+        extra = dot3(split(extra), ef) * w_rest
+        extra = dot3(split(extra), eb)
+        for half in range(2):
+            group = 2 * pair + half
+            at = 64 * half
+            tiles = []
+            for h in range(2):
+                tile = mains[half][:, h * LANES : (h + 1) * LANES]
+                tiles.append(jnp.where(lane < 120, tile, turn(extra, 120 - at - 8 * h)))
+            value = dot3(cb, split(jnp.concatenate(tiles, axis=1)))
+            for h in range(2):
+                main_ref[h, group * size : (group + 1) * size, :] = value[:, h * LANES : (h + 1) * LANES]
+            inside = (lane >= 32 * group) & (lane < 32 * group + 24)
+            rest_back = jnp.where(inside, turn(extra, 32 * group - at - 16), rest_back)
+    rest = dot3(cb, split(rest_back))
+    for group in range(groups):
+        rest_ref[group * size : (group + 1) * size, :] = jnp.where(lane < 24, turn(rest, -32 * group), 0.0)
 
     for first in range(0, STATES, 4):
         for second in range(0, first + 4, 4):
@@ -304,12 +358,14 @@
                 out_ref[pl.ds(s * 1000 + u * 2 + c, 20, stride=50), :] = value
 
 
-def call(kernel, outs, scratch, cost):
+def call(kernel, outs, scratch, cost, places="v", limit=SMALL_VMEM):
+    spaces = {"v": pltpu.VMEM, "h": pltpu.HBM}
     return pl.pallas_call(
         kernel,
         out_shape=outs,
+        in_specs=[pl.BlockSpec(memory_space=spaces[p]) for p in places],
         scratch_shapes=scratch,
-        compiler_params=pltpu.CompilerParams(vmem_limit_bytes=SMALL_VMEM),
+        compiler_params=pltpu.CompilerParams(vmem_limit_bytes=limit),
         cost_estimate=pl.CostEstimate(flops=cost, bytes_accessed=1 << 20, transcendentals=0),
     )
 
@@ -331,41 +387,46 @@
 def body(states, membrane_step, cavity_forward, coupling, membrane_forward, cavity_back, membrane_back):
     panel, levels, joint = states.shape
     everyone = ("state", "basis")
-    linear = states.reshape(panel, levels, joint // LANES, LANES)
+    by_tile = Layout(major_to_minor=(0, 2, 1, 3))
+    linear = with_layout_constraint(states.reshape(panel, levels, joint // LANES, LANES), by_tile)
     linear = jnp.swapaxes(linear, 1, 2).reshape(-1, LANES)
     blocks = shape(256 * ROWS, LANES)
     send = call(
         head_kernel,
         blocks,
-        [pltpu.VMEM((48, 13 * LANES), F32), pltpu.VMEM((2, M, LANES), F32)],
+        [
+            pltpu.VMEM((2000, LANES), F32),
+            pltpu.VMEM((M, M), F32),
+            pltpu.VMEM((48, 13 * LANES), F32),
+            pltpu.VMEM((2, M, LANES), F32),
+            pltpu.SemaphoreType.DMA((3,)),
+        ],
         1 << 20,
+        "hh",
+        LARGE_VMEM,
     )(linear, membrane_step)
-    size = GROUP * LEVELS
-    cf, cb, mf, mb, w = call(
-        operands_kernel,
-        (
-            shape(2, size, size, dtype=BF16),
-            shape(2, size, size, dtype=BF16),
-            shape(2, WIDE, WIDE, dtype=BF16),
-            shape(2, WIDE, WIDE, dtype=BF16),
-            shape(LEVELS, WIDE),
-        ),
-        [],
-        1 << 27,
-    )(cavity_forward, coupling, membrane_forward, cavity_back, membrane_back)
+    squares = [shape(2, LANES, LANES, dtype=BF16)] * 6
+    operands = call(operands_kernel, (*squares, shape(2, LEVELS, LANES)), [], 1 << 27, "vvvvv")(
+        cavity_forward, coupling, membrane_forward, cavity_back, membrane_back
+    )
     recv = exchange(send, everyone)
     main, rest, gram = call(
         step_kernel,
         (shape(2, STATES * LEVELS, LANES), shape(STATES * LEVELS, LANES), shape(64, LANES)),
         [pltpu.VMEM((STATES * STATES, LANES), F32)],
         1 << 30,
-    )(recv, cf, cb, mf, mb, w)
+        "vvvvvvvv",
+    )(recv, *operands)
     gram = lax.all_to_all(gram.reshape(32, 2, LANES), "basis", split_axis=0, concat_axis=0, tiled=True)
     gram = jnp.broadcast_to(jnp.sum(gram, axis=0, keepdims=True), (8, 2, LANES))
     gram = lax.all_to_all(gram, "state", split_axis=0, concat_axis=0, tiled=True)
     scale = 1.0 / float(LEVELS * joint)
     send = call(
-        lambda *refs: mix_kernel(scale, *refs), blocks, [pltpu.VMEM((STATES * STATES, LANES), F32)], 1 << 27
+        lambda *refs: mix_kernel(scale, *refs),
+        blocks,
+        [pltpu.VMEM((STATES * STATES, LANES), F32)],
+        1 << 27,
+        "vvv",
     )(gram.reshape(16, LANES), main, rest)
     recv = exchange(send, everyone)
     out = call(
@@ -375,7 +436,7 @@
         1 << 20,
     )(recv)
     out = out.reshape(panel, joint // LANES, levels, LANES)
-    return jnp.swapaxes(out, 1, 2).reshape(panel, levels, joint)
+    return with_layout_constraint(jnp.swapaxes(out, 1, 2), by_tile).reshape(panel, levels, joint)
 
 
 def solution(mesh):

time: 134 us -> 126 us (0.940)
  local copies, waits for them, and re-layouts: 9.38 us -> 0.12 us
  waiting for transfers between devices: 28.4 us -> 32.1 us
  Pallas kernels: 18 us -> 16.4 us
    unnamed x25 -> x11, local copies, waits for them, and re-layouts: 5.45 us -> 0.11 us
    all_to_all x1, waiting for transfers between devices: 28.4 us -> 32.1 us  [exchange(): value = lax.all_to_all(value, axes, split_axis=0, concat_axis=0, tiled=True)]
    reshape x3 -> x0, local copies, waits for them, and re-layouts: 3.4 us -> none  [the longest x1 1.88 us: body(): linear = states.reshape(panel, levels, joint // LANES, LANES)]
    pallas_call x1, Pallas kernels: 8.18 us -> 5.91 us  [body(): call(step_kernel, (shape(2, STATES * LEVELS, LANES), shape(STATES * LEVEL...]
  transfers between devices with their start and end apart: 1 -> 1, of which waited for: 1 -> 1; matrix products, arithmetic and copies ran while one was open for 0% -> 0% of each run, Pallas kernels for 2% -> 1%
where the time goes in v2:
time: 126 us
  blocking collectives  61.3 us (49%)
  waiting for transfers between devices  32.1 us (25%)
  Pallas kernels  16.4 us (13%)
  starting transfers between devices  15.7 us (12%)
    all_to_all x1, blocking collectives, exchange(): value = lax.all_to_all(value, axes, split_axis=0, concat_axis=0, tiled=True)  39.7 us
    all_to_all x1, waiting for transfers between devices, exchange(): value = lax.all_to_all(value, axes, split_axis=0, concat_axis=0, tiled=True)  32.1 us
    all_to_all x1, starting transfers between devices, exchange(): value = lax.all_to_all(value, axes, split_axis=0, concat_axis=0, tiled=True)  15.7 us
    all_to_all x1, blocking collectives, body(): lax.all_to_all(gram.reshape(32, 2, LANES), 'basis', split_axis=0, concat_...  12.7 us
    all_to_all x1, blocking collectives, body(): lax.all_to_all(gram, 'state', split_axis=0, concat_axis=0, tiled=True)  8.93 us
    pallas_call x1, Pallas kernels, body(): call(step_kernel, (shape(2, STATES * LEVELS, LANES), shape(STATES * LEVEL...  5.91 us
    pallas_call x1, Pallas kernels, body(): call(head_kernel, blocks, [pltpu.VMEM((2000, LANES), F32), pltpu.VMEM((M,...  3.97 us
    pallas_call x1, Pallas kernels, body(): call(lambda *refs: mix_kernel(scale, *refs), blocks, [pltpu.VMEM((STATES...  3.18 us
  transfers between devices with their start and end apart: 1, of which 1 were waited for; matrix products, arithmetic and copies ran while one was open for 0% of the time, Pallas kernels for 1%

profile of v2, /device:TPU:1, one launch (start us, length us, event | category | flops | bytes accessed | tf_op | source)
XLA Modules:
  0.0 125.8 jit_solution(3544875620809806853)
XLA Ops:
  0.0 4.0 %shard_map.73 = f32[2304,128]{1,0:T(8,128)} custom-call(f32[2000,128]{1,0:T(8,128)} %bitcast.22, f32[40,40]{1,0:T(8,128)} %step_hbm.1), custom_call_target="tpu_custom_call" | custom-call | flops 1048576 | bytes 1048576 | tf_op jit(solution)/shard_map/pallas_call | solution.py:394
  4.0 0.0 copy-start.4
  4.0 0.0 copy-start
  4.0 0.0 copy-start.1
  4.0 0.0 copy-start.2
  4.0 0.0 copy-start.3
  4.0 15.7 %all-to-all-start = ((f32[256,1,1152]{2,1,0:T(1,128)}), f32[256,1,1152]{2,1,0:T(1,128)S(1)}, u32[]{:S(2)}, u32[]{:S(2)}) async-start(f32[256,1,1152]{2,1,0:T(1,128)} %bitcast.21), calls=%async_computation | async-start | bytes 2359296 | tf_op jit(solution)/shard_map/all_to_all | solution.py:383
  19.7 0.0 copy-done.4
  19.7 0.1 copy.10.coupling_ref
  19.8 0.0 copy-done
  19.8 0.0 copy-done.1
  19.8 0.0 copy-done.2
  19.8 0.0 copy-done.3
  19.8 1.1 shard_map.74
  20.9 32.1 %all-to-all-done = f32[256,1,1152]{2,1,0:T(1,128)S(1)} async-done(((f32[256,1,1152]{2,1,0:T(1,128)}), f32[256,1,1152]{2,1,0:T(1,128)S(1)}, u32[]{:S(2)}, u32[]{:S(2)}) %all-to-all-start) | async-done | bytes 1179680 | tf_op jit(solution)/shard_map/all_to_all | solution.py:383
  53.0 5.9 %shard_map.75 = (f32[2,1024,128]{2,1,0:T(8,128)S(1)}, f32[1024,128]{1,0:T(8,128)S(1)}, f32[64,128]{1,0:T(8,128)S(1)}) custom-call(f32[2304,128]{1,0:T(8,128)S(1)} %bitcast.18, bf16[2,128,128]{2,1,0:T(8,128)(2,1)S(1)} %get-tuple-element.15.cf_ref, bf16[2,128,128]{2,1,0:T(8,128)(2,1)S(1)} %get-tuple-element.16.cb_ref, ...), custom_call_target="tpu_custom_call" | custom-call | flops 1073741824 | bytes 1048576 | tf_op jit(solution)/shard_map/pallas_call | solution.py:413
  58.9 12.7 %all_to_all.20 = f32[32,2,128]{2,1,0:T(2,128)S(1)} all-to-all(f32[32,2,128]{2,1,0:T(2,128)S(1)} %bitcast.20), channel_id=1, replica_groups=mesh['state'=8,'basis'=32] {'basis'}, dimensions={0} | all-to-all | bytes 65536 | tf_op jit(solution)/shard_map/all_to_all | solution.py:420
  71.6 8.9 %all_to_all.21 = f32[8,2,128]{2,1,0:T(2,128)S(1)} all-to-all(f32[8,2,128]{2,1,0:T(2,128)S(1)} %broadcast_in_dim.2), channel_id=1, replica_groups=mesh['state'=8,'basis'=32] {'state'}, dimensions={0} | all-to-all | bytes 16384 | tf_op jit(solution)/shard_map/all_to_all | solution.py:422
  80.6 3.2 %shard_map.76 = f32[2304,128]{1,0:T(8,128)S(1)} custom-call(f32[16,128]{1,0:T(8,128)S(1)} %bitcast.19, f32[2,1024,128]{2,1,0:T(8,128)S(1)} %get-tuple-element.23.refs_1_, f32[1024,128]{1,0:T(8,128)S(1)} %get-tuple-element.24.refs_2_), custom_call_target="tpu_custom_call" | custom-call | flops 134217728 | bytes 1048576 | tf_op jit(solution)/shard_map/pallas_call | solution.py:424
  83.7 39.7 %all_to_all.22 = f32[256,1,1152]{2,1,0:T(1,128)S(1)} all-to-all(f32[256,1,1152]{2,1,0:T(1,128)S(1)} %bitcast.17), channel_id=1, replica_groups=mesh['state'=8,'basis'=32] {'state','basis'}, dimensions={0} | all-to-all | bytes 2359296 | tf_op jit(solution)/shard_map/all_to_all | solution.py:383
  123.5 2.3 %shard_map.77 = f32[2000,128]{1,0:T(8,128)} custom-call(f32[2304,128]{1,0:T(8,128)S(1)} %bitcast.16), custom_call_target="tpu_custom_call" | custom-call | flops 1048576 | bytes 1048576 | tf_op jit(solution)/shard_map/pallas_call | solution.py:432
  (2 shorter events, 0.1 us)
Async XLA Ops:
  4.0 15.7 %copy-start.4 = (f32[64,40]{0,1:T(8,128)S(1)}, f32[64,40]{0,1:T(8,128)}, u32[]{:S(2)}) copy-start(f32[64,40]{0,1:T(8,128)} %param.10) | copy-start | bytes 30724
  4.0 15.8 %copy-start = (f32[64,64]{1,0:T(8,128)S(1)}, f32[64,64]{1,0:T(8,128)}, u32[]{:S(2)}) copy-start(f32[64,64]{1,0:T(8,128)} %forward_ref.1) | copy-start | bytes 49156
  4.0 15.8 %copy-start.1 = (f32[64,64]{1,0:T(8,128)S(1)}, f32[64,64]{1,0:T(8,128)}, u32[]{:S(2)}) copy-start(f32[64,64]{1,0:T(8,128)} %back_ref.1) | copy-start | bytes 49156
  4.0 15.8 %copy-start.2 = (f32[40,40]{1,0:T(8,128)S(1)}, f32[40,40]{1,0:T(8,128)}, u32[]{:S(2)}) copy-start(f32[40,40]{1,0:T(8,128)} %mem_forward_ref.1) | copy-start | bytes 19204
  4.0 15.8 %copy-start.3 = (f32[40,40]{1,0:T(8,128)S(1)}, f32[40,40]{1,0:T(8,128)}, u32[]{:S(2)}) copy-start(f32[40,40]{1,0:T(8,128)} %mem_back_ref.1) | copy-start | bytes 19204
  4.0 48.9 %all-to-all-start = ((f32[256,1,1152]{2,1,0:T(1,128)}), f32[256,1,1152]{2,1,0:T(1,128)S(1)}, u32[]{:S(2)}, u32[]{:S(2)}) async-start(f32[256,1,1152]{2,1,0:T(1,128)} %bitcast.21), calls=%async_computation | async-start | bytes 2359296 | tf_op jit(solution)/shard_map/all_to_all | solution.py:383

commit v3 on v2

--- a/solution.py
+++ b/solution.py
@@ -4,6 +4,7 @@
 from jax.experimental.layout import Layout, with_layout_constraint
 from jax.experimental import pallas as pl
 from jax.experimental.pallas import tpu as pltpu
+from jax.sharding import Mesh
 from jax.sharding import PartitionSpec as P
 
 ROWS = 9
@@ -38,7 +39,12 @@
     return out + jnp.dot(ah, bh, preferred_element_type=F32)
 
 
-def head_kernel(states_hbm, step_hbm, send_ref, states_ref, step_ref, x_ref, extra_ref, sems):
+def turn(value, shift):
+    shift = shift % LANES
+    return pltpu.roll(value, shift, 1) if shift else value
+
+
+def head_kernel(states_hbm, step_hbm, send_hbm, send_ref, states_ref, step_ref, x_ref, tile_ref, sems):
     step_copy = pltpu.make_async_copy(step_hbm, step_ref, sems.at[2])
     step_copy.start()
     copies = []
@@ -46,8 +52,9 @@
         part = pl.ds(s * 1000, 1000)
         copies.append(pltpu.make_async_copy(states_hbm.at[part], states_ref.at[part], sems.at[s]))
         copies[-1].start()
-    x_ref[...] = jnp.zeros(x_ref.shape, F32)
-    extra_ref[...] = jnp.zeros(extra_ref.shape, F32)
+    for e in range(4):
+        for row in (16, 40):
+            x_ref[e, row : row + 8, :] = jnp.zeros((8, 13 * LANES), F32)
     send_ref[pl.ds(80 * ROWS + 8, 176, stride=ROWS), :] = jnp.zeros((176, LANES), F32)
     row, col = iota((M, M), 0), iota((M, M), 1)
     order = (col == jnp.where(row < 20, 2 * row, 2 * row - 39)).astype(F32)
@@ -55,7 +62,8 @@
     even = (col < 20) & (row == 2 * col)
     odd = (col >= 24) & (col < 44) & (row == 2 * col - 47)
     step_copy.wait()
-    step = exact_dot(exact_dot(order, step_ref[...]), (even | odd).astype(F32))
+    step = split(exact_dot(exact_dot(order, step_ref[...]), (even | odd).astype(F32)))
+
     lane = iota((M, LANES), 1)
     lane20 = iota((20, LANES), 1)
     for s in range(2):
@@ -67,68 +75,66 @@
                 return states_ref[pl.ds(s * 1000 + u * 2 + c, 20, stride=50), :]
 
             for v in range(13):
-                x_ref[0:20, v * LANES : (v + 1) * LANES] = tile_in(v)
+                x_ref[e, 0:20, v * LANES : (v + 1) * LANES] = tile_in(v)
                 low = pltpu.roll(tile_in(12 + v), 64, 1)
                 high = pltpu.roll(tile_in(min(13 + v, 24)), 64, 1)
-                x_ref[24:44, v * LANES : (v + 1) * LANES] = jnp.where(lane20 < 64, low, high)
-            out = exact_dot(step, x_ref[...])
-            tiles = [out[:, v * LANES : (v + 1) * LANES] for v in range(13)]
-
-            def chunk(m):
-                if m == 0:
-                    return tiles[0]
-                return jnp.where(
-                    lane < 8 * m, pltpu.roll(tiles[m - 1], 8 * m, 1), pltpu.roll(tiles[m], 8 * m, 1)
-                )
-
-            last = chunk(12)
-            tail = last[32:40]
-            extras = [
-                pltpu.roll(tiles[12], LANES - 24, 1),
-                jnp.concatenate(
-                    [
-                        tail,
-                        pltpu.roll(tail, LANES - 40, 1),
-                        pltpu.roll(tail, LANES - 80, 1),
-                        jnp.zeros((16, LANES), F32),
-                    ],
-                    axis=0,
-                ),
-            ]
-            for m in range(12):
-                g, h = m // 2, m % 2
-                spare = pltpu.roll(extras[g], 120 - 8 * h, 1) if g < 2 else jnp.zeros((M, LANES), F32)
-                block = jnp.where(lane < 120, chunk(m), spare)
+                x_ref[e, 24:44, v * LANES : (v + 1) * LANES] = jnp.where(lane20 < 64, low, high)
+            tile_ref[e] = dot3(step, split(x_ref[e]))
+
+    def tile(e, v):
+        return tile_ref[e, :, v * LANES : (v + 1) * LANES]
+
+    def chunk(e, m):
+        if m == 0:
+            return tile(e, 0)
+        return jnp.where(lane < 8 * m, turn(tile(e, m - 1), 8 * m), turn(tile(e, m), 8 * m))
+
+    copies = []
+    for g in (6, 0, 1, 2, 3, 4, 5):
+        extra = jnp.zeros((M, LANES), F32)
+        for e in range(4):
+            if g == 6:
+                last = jnp.where(lane < 120, chunk(e, 12), 0.0)
+                for h in range(2):
+                    block = last[16 * h : 16 * h + 16]
+                    send_ref[pl.ds(240 * ROWS + h * 4 + e, 16, stride=ROWS), :] = block
+                continue
+            if g == 0:
+                seventh = turn(tile(e, 12), -24)
+            elif g == 1:
+                tail = chunk(e, 12)[32:40]
+                tails = [tail, turn(tail, -40), turn(tail, -80), jnp.zeros((16, LANES), F32)]
+                seventh = jnp.concatenate(tails, axis=0)
+            for h in range(2):
+                spare = turn(seventh, 120 - 8 * h) if g < 2 else 0.0
+                block = jnp.where(lane < 120, chunk(e, 2 * g + h), spare)
                 send_ref[pl.ds(g * M * ROWS + h * 4 + e, M, stride=ROWS), :] = block
-            last = jnp.where(lane < 120, last, 0.0)
-            for h in range(2):
-                send_ref[pl.ds(240 * ROWS + h * 4 + e, 16, stride=ROWS), :] = last[16 * h : 16 * h + 16]
-            inside = (lane >= 32 * e) & (lane < 32 * e + 24)
-            for g in range(2):
-                moved = pltpu.roll(extras[g], (32 * e - 16) % LANES, 1)
-                extra_ref[g] += jnp.where(inside, moved, 0.0)
-    for g in range(2):
-        send_ref[pl.ds(g * M * ROWS + 8, M, stride=ROWS), :] = extra_ref[g]
+            if g < 2:
+                inside = (lane >= 32 * e) & (lane < 32 * e + 24)
+                extra = jnp.where(inside, turn(seventh, 32 * e - 16), extra)
+        if g < 2:
+            send_ref[pl.ds(g * M * ROWS + 8, M, stride=ROWS), :] = extra
+        part = pl.ds(g * M * ROWS, (M if g < 6 else 16) * ROWS)
+        copies.append(pltpu.make_async_copy(send_ref.at[part], send_hbm.at[part], sems.at[3 + g]))
+        copies[-1].start()
+    for copy in copies:
+        copy.wait()
 
 
 def operands_kernel(
     forward_ref, coupling_ref, mem_forward_ref, back_ref, mem_back_ref,
     cf_ref, cb_ref, mf_ref, mb_ref, ef_ref, eb_ref, w_ref,
 ):
-    size = 2 * LEVELS
-    same = (iota((size, size), 0) >> 6) == (iota((size, size), 1) >> 6)
-    tall = (iota((size, LEVELS), 1) == (iota((size, LEVELS), 0) & 63)).astype(F32)
-    wide = (iota((LEVELS, size), 0) == (iota((LEVELS, size), 1) & 63)).astype(F32)
-
     def level_of(p):
-        return 2 * (p & 31) + ((p >> 5) & 1)
-
-    tall_level = (iota((size, LEVELS), 1) == level_of(iota((size, LEVELS), 0))).astype(F32)
-    wide_level = (iota((LEVELS, size), 0) == level_of(iota((LEVELS, size), 1))).astype(F32)
-    forward = exact_dot(tall, exact_dot(forward_ref[...], wide_level))
-    back = exact_dot(tall_level, exact_dot(back_ref[...], wide))
+        return 4 * (p & 15) + 2 * ((p >> 4) & 1) + ((p >> 5) & 1)
+
+    row, lane = iota((LEVELS, 4 * LEVELS), 0), iota((LEVELS, 4 * LEVELS), 1)
+    forward = exact_dot(forward_ref[...], (row == level_of(lane & 63)).astype(F32))
+    ordered = (iota((LEVELS, LEVELS), 1) == level_of(iota((LEVELS, LEVELS), 0))).astype(F32)
+    back = exact_dot(exact_dot(ordered, back_ref[...]), (row == (lane & 63)).astype(F32))
     for ref, value in ((cf_ref, forward), (cb_ref, back)):
-        ref[0], ref[1] = split(jnp.where(same, value, 0.0))
+        high, low = (part.astype(F32) for part in split(value))
+        ref[...] = jnp.where(lane < 128, high, jnp.where(lane < 192, low, 0.0)).astype(BF16)
 
     def threes(lane):
         third = (lane >= 40).astype(jnp.int32) + (lane >= 80).astype(jnp.int32)
@@ -152,23 +158,41 @@
         w_ref[n] = exact_dot(coupling_ref[...], across)
 
 
-def twice(block):
-    zero = jnp.zeros_like(block)
-    return jnp.concatenate(
-        [jnp.concatenate([block, zero], axis=1), jnp.concatenate([zero, block], axis=1)], axis=0
-    )
-
-
-def turn(value, shift):
-    shift = shift % LANES
-    return pltpu.roll(value, shift, 1) if shift else value
+def cavity(matrix, value):
+    high, low = split(value)
+    out = []
+    for row in range(0, value.shape[0], LEVELS):
+        h, l = high[row : row + LEVELS], low[row : row + LEVELS]
+        stacked = jnp.concatenate([h, l, h, h], axis=0)
+        out.append(jnp.dot(matrix, stacked, preferred_element_type=F32))
+    return jnp.concatenate(out, axis=0)
+
+
+def doubled(ref):
+    high, low = ref[0], ref[1]
+    left = jnp.concatenate([high, high], axis=0)
+    right = jnp.concatenate([low, jnp.zeros_like(low)], axis=0)
+    return jnp.concatenate([left, right], axis=1)
+
+
+def membrane(value, matrix):
+    out = []
+    for lane in range(0, value.shape[1], LANES):
+        high, low = split(value[:, lane : lane + LANES])
+        both = jnp.dot(jnp.concatenate([high, low], axis=1), matrix, preferred_element_type=F32)
+        out.append(both[:, :LANES] + both[:, LANES:])
+    return jnp.concatenate(out, axis=1) if len(out) > 1 else out[0]
+
+
+def flat_place(s, t):
+    return (s // 8) * LANES + (-s % 8) * STATES + t
 
 
 def step_kernel(
     recv_ref, cf_ref, cb_ref, mf_ref, mb_ref, ef_ref, eb_ref, w_ref, main_ref, rest_ref, gram_ref, rows_ref
 ):
-    cf, cb, mf, mb = ((twice(ref[0]), twice(ref[1])) for ref in (cf_ref, cb_ref, mf_ref, mb_ref))
-    ef, eb = (ef_ref[0], ef_ref[1]), (eb_ref[0], eb_ref[1])
+    cf, cb = cf_ref[...], cb_ref[...]
+    mf, mb, ef, eb = (doubled(ref) for ref in (mf_ref, mb_ref, ef_ref, eb_ref))
     w_half = jnp.concatenate([w_ref[0]] * GROUP, axis=0)
     w_main = jnp.concatenate([w_half, w_half], axis=1)
     w_rest = jnp.concatenate([w_ref[1]] * GROUP, axis=0)
@@ -184,7 +208,7 @@
             for g in range(2, -1, -1):
                 value = jnp.where(lane < 32 * g + 32, turn(sevenths[g], 32 * (g - e)), value)
             parts.append(jnp.where((lane & 31) < 24, value, 0.0))
-    rest = dot3(cf, split(jnp.concatenate(parts, axis=0)))
+    rest = cavity(cf, jnp.concatenate(parts, axis=0))
 
     lane = iota((size, LANES), 1)
     rest_back = jnp.zeros((size, LANES), F32)
@@ -198,15 +222,15 @@
                 for e in range(4):
                     tiles = [recv_ref[pl.ds(z * 32 * ROWS + h * 4 + e, 32, stride=ROWS), :] for h in range(2)]
                     parts.append(jnp.concatenate(tiles, axis=1))
-            value = dot3(cf, split(jnp.concatenate(parts, axis=0)))
+            value = cavity(cf, jnp.concatenate(parts, axis=0))
             at = 64 * half
             moved = jnp.where(lane < at + 16, turn(value[:, LANES:], at + 16), turn(rest, at + 16 - 32 * group))
             moved = jnp.where(lane < at + 8, turn(value[:, :LANES], at + 8), moved)
             extra = jnp.where((lane >= at) & (lane < at + 40), moved, extra)
-            value = dot3(split(value), mf) * w_main
-            mains.append(dot3(split(value), mb))
-        extra = dot3(split(extra), ef) * w_rest
-        extra = dot3(split(extra), eb)
+            value = membrane(value, mf) * w_main
+            mains.append(membrane(value, mb))
+        extra = membrane(extra, ef) * w_rest
+        extra = membrane(extra, eb)
         for half in range(2):
             group = 2 * pair + half
             at = 64 * half
@@ -214,12 +238,12 @@
             for h in range(2):
                 tile = mains[half][:, h * LANES : (h + 1) * LANES]
                 tiles.append(jnp.where(lane < 120, tile, turn(extra, 120 - at - 8 * h)))
-            value = dot3(cb, split(jnp.concatenate(tiles, axis=1)))
+            value = cavity(cb, jnp.concatenate(tiles, axis=1))
             for h in range(2):
                 main_ref[h, group * size : (group + 1) * size, :] = value[:, h * LANES : (h + 1) * LANES]
             inside = (lane >= 32 * group) & (lane < 32 * group + 24)
             rest_back = jnp.where(inside, turn(extra, 32 * group - at - 16), rest_back)
-    rest = dot3(cb, split(rest_back))
+    rest = cavity(cb, rest_back)
     for group in range(groups):
         rest_ref[group * size : (group + 1) * size, :] = jnp.where(lane < 24, turn(rest, -32 * group), 0.0)
 
@@ -238,14 +262,14 @@
                     sums = tuple(sums[p * 4 + q] + a[p] * b[q] for p in range(4) for q in range(4))
                 return sums
 
-            sums = lax.fori_loop(0, 8, add, (jnp.zeros((8, LANES), F32),) * 16)
+            sums = lax.fori_loop(0, 8, add, (jnp.zeros((8, LANES), F32),) * 16, unroll=True)
             for p in range(4):
                 for q in range(4):
                     total = jnp.sum(sums[p * 4 + q], axis=0, keepdims=True)
-                    at = (first + p) * STATES + second + q
+                    at = flat_place(first + p, second + q)
                     rows_ref[at : at + 1, :] = total
                     if first != second:
-                        at = (second + q) * STATES + first + p
+                        at = flat_place(second + q, first + p)
                         rows_ref[at : at + 1, :] = total
     flat = lax.dot_general(
         jnp.ones((32, LANES), F32), rows_ref[...], (((1,), (1,)), ((), ())), precision=HIGHEST,
@@ -260,24 +284,21 @@
     for z in range(1, 8):
         gram = gram + gram_ref[2 * z : 2 * z + 2, :]
     gram = gram * scale
-    flat = jnp.concatenate([gram[0:1], gram[1:2]], axis=1)
-    row, col = iota((STATES, 2 * LANES), 0), iota((STATES, 2 * LANES), 1)
-    spread = jnp.where((col >> 4) == row, flat, 0.0)
-    row, col = iota((2 * LANES, LANES), 0), iota((2 * LANES, LANES), 1)
-    square = exact_dot(spread, ((row & 15) == col).astype(F32))
+    square = [
+        pltpu.roll(jnp.broadcast_to(gram[h : h + 1], (8, LANES)), 0, 1, stride=16, stride_axis=0)
+        for h in range(2)
+    ]
     row, col = iota((STATES, LANES), 0), iota((STATES, LANES), 1)
-    work = square + (col == row + STATES).astype(F32)
+    work = jnp.where(col < STATES, jnp.concatenate(square, axis=0), (col == row + STATES).astype(F32))
     for j in range(STATES - 1):
         pivot = work[j : j + 1, :]
-        factor = work[:, j : j + 1] / work[j : j + 1, j : j + 1]
-        work = work - jnp.where(row > j, factor, 0.0) * pivot
+        pivot = pivot * (1.0 / jnp.broadcast_to(pivot[:, j : j + 1], (1, LANES)))
+        work = work - jnp.where(row > j, work[:, j : j + 1], 0.0) * pivot
     diagonal = jnp.sum(jnp.where(col == row, work, 0.0), axis=1, keepdims=True)
     inverse = work / jnp.sqrt(diagonal)
-    row, col = iota((STATES * STATES, STATES), 0), iota((STATES * STATES, STATES), 1)
-    repeated = exact_dot(((row >> 4) == col).astype(F32), inverse)
-    row, col = iota((STATES * STATES, LANES), 0), iota((STATES * STATES, LANES), 1)
-    picked = jnp.where(col == (row & 15) + STATES, repeated, 0.0)
-    coef_ref[...] = exact_dot(picked, jnp.ones((LANES, LANES), F32))
+    for st in range(STATES):
+        column = jnp.broadcast_to(inverse[:, STATES + st : STATES + st + 1], (STATES, LANES))
+        coef_ref[st * STATES : (st + 1) * STATES, :] = column
 
     lane = iota((8, LANES), 1)
 
@@ -286,7 +307,7 @@
         for t in range(STATES):
             sums = [None, None]
             for st in range(t + 1):
-                factor = coef_ref[t * STATES + st : t * STATES + st + 1, :]
+                factor = coef_ref[st * STATES + t : st * STATES + t + 1, :]
                 for n in range(2):
                     term = factor * values[st][n]
                     sums[n] = term if sums[n] is None else sums[n] + term
@@ -315,16 +336,18 @@
                 send_ref[pl.ds((z * 32 + start) * ROWS + 8, 8, stride=ROWS), :] = seventh
         return carry
 
-    lax.fori_loop(0, 4, tile, 0)
-
-
-def tail_kernel(recv_ref, out_ref, chunk_ref, tile_ref):
+    lax.fori_loop(0, 4, tile, 0, unroll=2)
+
+
+def tail_kernel(recv_ref, out_hbm, out_ref, chunks_ref, tiles_ref, sems):
+    copies = []
     lane = iota((M, LANES), 1)
     lane8 = iota((8, LANES), 1)
     lane20 = iota((20, LANES), 1)
     for s in range(2):
         for c in range(2):
             e = s * 2 + c
+            chunk_ref, tile_ref = chunks_ref.at[e], tiles_ref.at[e]
             for m in range(12):
                 g, h = m // 2, m % 2
                 chunk_ref[m] = recv_ref[pl.ds(g * M * ROWS + h * 4 + e, M, stride=ROWS), :]
@@ -356,14 +379,20 @@
                     high = pltpu.roll(tile_ref[u - 12, 20:40], 64, 1)
                     value = jnp.where(lane20 < 64, low, high)
                 out_ref[pl.ds(s * 1000 + u * 2 + c, 20, stride=50), :] = value
-
-
-def call(kernel, outs, scratch, cost, places="v", limit=SMALL_VMEM):
+        part = pl.ds(s * 1000, 1000)
+        copies.append(pltpu.make_async_copy(out_ref.at[part], out_hbm.at[part], sems.at[s]))
+        copies[-1].start()
+    for copy in copies:
+        copy.wait()
+
+
+def call(kernel, outs, scratch, cost, places="v", limit=SMALL_VMEM, out_place="v"):
     spaces = {"v": pltpu.VMEM, "h": pltpu.HBM}
     return pl.pallas_call(
         kernel,
         out_shape=outs,
         in_specs=[pl.BlockSpec(memory_space=spaces[p]) for p in places],
+        out_specs=jax.tree.map(lambda _: pl.BlockSpec(memory_space=spaces[out_place]), outs),
         scratch_shapes=scratch,
         compiler_params=pltpu.CompilerParams(vmem_limit_bytes=limit),
         cost_estimate=pl.CostEstimate(flops=cost, bytes_accessed=1 << 20, transcendentals=0),
@@ -386,7 +415,7 @@
 
 def body(states, membrane_step, cavity_forward, coupling, membrane_forward, cavity_back, membrane_back):
     panel, levels, joint = states.shape
-    everyone = ("state", "basis")
+    everyone = ("state", "core", "plane")
     by_tile = Layout(major_to_minor=(0, 2, 1, 3))
     linear = with_layout_constraint(states.reshape(panel, levels, joint // LANES, LANES), by_tile)
     linear = jnp.swapaxes(linear, 1, 2).reshape(-1, LANES)
@@ -395,18 +424,21 @@
         head_kernel,
         blocks,
         [
+            pltpu.VMEM((256 * ROWS, LANES), F32),
             pltpu.VMEM((2000, LANES), F32),
             pltpu.VMEM((M, M), F32),
-            pltpu.VMEM((48, 13 * LANES), F32),
-            pltpu.VMEM((2, M, LANES), F32),
-            pltpu.SemaphoreType.DMA((3,)),
+            pltpu.VMEM((4, 48, 13 * LANES), F32),
+            pltpu.VMEM((4, M, 13 * LANES), F32),
+            pltpu.SemaphoreType.DMA((10,)),
         ],
         1 << 20,
         "hh",
         LARGE_VMEM,
+        "h",
     )(linear, membrane_step)
-    squares = [shape(2, LANES, LANES, dtype=BF16)] * 6
-    operands = call(operands_kernel, (*squares, shape(2, LEVELS, LANES)), [], 1 << 27, "vvvvv")(
+    wides = [shape(LEVELS, 4 * LEVELS, dtype=BF16)] * 2
+    squares = [shape(2, LANES, LANES, dtype=BF16)] * 4
+    operands = call(operands_kernel, (*wides, *squares, shape(2, LEVELS, LANES)), [], 1 << 27, "vvvvv")(
         cavity_forward, coupling, membrane_forward, cavity_back, membrane_back
     )
     recv = exchange(send, everyone)
@@ -417,7 +449,7 @@
         1 << 30,
         "vvvvvvvv",
     )(recv, *operands)
-    gram = lax.all_to_all(gram.reshape(32, 2, LANES), "basis", split_axis=0, concat_axis=0, tiled=True)
+    gram = lax.all_to_all(gram.reshape(32, 2, LANES), ("plane", "core"), split_axis=0, concat_axis=0, tiled=True)
     gram = jnp.broadcast_to(jnp.sum(gram, axis=0, keepdims=True), (8, 2, LANES))
     gram = lax.all_to_all(gram, "state", split_axis=0, concat_axis=0, tiled=True)
     scale = 1.0 / float(LEVELS * joint)
@@ -432,14 +464,22 @@
     out = call(
         tail_kernel,
         shape(2000, LANES),
-        [pltpu.VMEM((14, M, LANES), F32), pltpu.VMEM((13, M, LANES), F32)],
+        [
+            pltpu.VMEM((2000, LANES), F32),
+            pltpu.VMEM((4, 14, M, LANES), F32),
+            pltpu.VMEM((4, 13, M, LANES), F32),
+            pltpu.SemaphoreType.DMA((2,)),
+        ],
         1 << 20,
+        out_place="h",
     )(recv)
     out = out.reshape(panel, joint // LANES, levels, LANES)
     return with_layout_constraint(jnp.swapaxes(out, 1, 2), by_tile).reshape(panel, levels, joint)
 
 
 def solution(mesh):
-    in_specs = (P("state", "basis", None), P(), P(), P(), P(), P(), P())
-    out_specs = P("state", "basis", None)
-    return jax.shard_map(body, mesh=mesh, in_specs=in_specs, out_specs=out_specs, check_vma=False)
+    states = mesh.shape["state"]
+    cores = Mesh(mesh.devices.reshape(states, -1, 2), ("state", "plane", "core"))
+    out_specs = P("state", ("plane", "core"), None)
+    in_specs = (out_specs, P(), P(), P(), P(), P(), P())
+    return jax.shard_map(body, mesh=cores, in_specs=in_specs, out_specs=out_specs, check_vma=False)

time: 126 us -> 123 us (0.976)
  Pallas kernels: 16.4 us -> 14 us
    pallas_call x1, Pallas kernels: 5.91 us -> 4.41 us  [body(): call(step_kernel, (shape(2, STATES * LEVELS, LANES), shape(STATES * LEVEL...]
where the time goes in v3:
time: 123 us
  blocking collectives  61.4 us (50%)
  waiting for transfers between devices  31.5 us (26%)
  starting transfers between devices  15.7 us (13%)
  Pallas kernels  14 us (11%)
    all_to_all x1, blocking collectives, exchange(): value = lax.all_to_all(value, axes, split_axis=0, concat_axis=0, tiled=True)  39.6 us
    all_to_all x1, waiting for transfers between devices, exchange(): value = lax.all_to_all(value, axes, split_axis=0, concat_axis=0, tiled=True)  31.5 us
    all_to_all x1, starting transfers between devices, exchange(): value = lax.all_to_all(value, axes, split_axis=0, concat_axis=0, tiled=True)  15.7 us
    all_to_all x1, blocking collectives, body(): lax.all_to_all(gram.reshape(32, 2, LANES), ('plane', 'core'), split_axis=...  12.8 us
    all_to_all x1, blocking collectives, body(): lax.all_to_all(gram, 'state', split_axis=0, concat_axis=0, tiled=True)  9.04 us
    pallas_call x1, Pallas kernels, body(): call(step_kernel, (shape(2, STATES * LEVELS, LANES), shape(STATES * LEVEL...  4.41 us
    pallas_call x1, Pallas kernels, body(): call(head_kernel, blocks, [pltpu.VMEM((256 * ROWS, LANES), F32), pltpu.VM...  3.75 us
  transfers between devices with their start and end apart: 1, of which 1 were waited for; matrix products, arithmetic and copies ran while one was open for 0% of the time, Pallas kernels for 1%

profile of v3, /device:TPU:1, one launch (start us, length us, event | category | flops | bytes accessed | tf_op | source)
XLA Modules:
  0.0 122.9 jit_solution(17938714823861256017)
XLA Ops:
  0.0 3.7 %shard_map.73 = f32[2304,128]{1,0:T(8,128)} custom-call(f32[2000,128]{1,0:T(8,128)} %bitcast.22, f32[40,40]{1,0:T(8,128)} %step_hbm.1), custom_call_target="tpu_custom_call" | custom-call | flops 1048576 | bytes 1048576 | tf_op jit(solution)/shard_map/pallas_call | solution.py:423
  3.8 0.0 copy-start.4
  3.8 0.0 copy-start
  3.8 0.0 copy-start.1
  3.8 0.0 copy-start.2
  3.8 0.0 copy-start.3
  3.8 15.7 %all-to-all-start = ((f32[256,1,1152]{2,1,0:T(1,128)}), f32[256,1,1152]{2,1,0:T(1,128)S(1)}, u32[]{:S(2)}, u32[]{:S(2)}) async-start(f32[256,1,1152]{2,1,0:T(1,128)} %bitcast.21), calls=%async_computation | async-start | bytes 2359296 | tf_op jit(solution)/shard_map/all_to_all | solution.py:412
  19.5 0.0 copy-done.4
  19.5 0.1 copy.10.coupling_ref
  19.6 0.0 copy-done
  19.6 0.0 copy-done.1
  19.6 0.0 copy-done.2
  19.6 0.0 copy-done.3
  19.6 1.3 %shard_map.74 = (bf16[64,256]{1,0:T(8,128)(2,1)S(1)}, bf16[64,256]{1,0:T(8,128)(2,1)S(1)}, bf16[2,128,128]{2,1,0:T(8,128)(2,1)S(1)}, bf16[2,128,128]{2,1,0:T(8,1...) custom-call(f32[64,64]{1,0:T(8,128)S(1)} %copy-done, ...), custom_call_target="tpu_custom_call" | custom-call | flops 134217728 | bytes 1048576 | tf_op jit(solution)/shard_map/pallas_call | solution.py:441
  20.9 31.5 %all-to-all-done = f32[256,1,1152]{2,1,0:T(1,128)S(1)} async-done(((f32[256,1,1152]{2,1,0:T(1,128)}), f32[256,1,1152]{2,1,0:T(1,128)S(1)}, u32[]{:S(2)}, u32[]{:S(2)}) %all-to-all-start) | async-done | bytes 1179680 | tf_op jit(solution)/shard_map/all_to_all | solution.py:412
  52.4 4.4 %shard_map.75 = (f32[2,1024,128]{2,1,0:T(8,128)S(1)}, f32[1024,128]{1,0:T(8,128)S(1)}, f32[64,128]{1,0:T(8,128)S(1)}) custom-call(f32[2304,128]{1,0:T(8,128)S(1)} %bitcast.18, bf16[64,256]{1,0:T(8,128)(2,1)S(1)} %get-tuple-element.15.cf_ref, bf16[64,256]{1,0:T(8,128)(2,1)S(1)} %get-tuple-element.16.cb_ref, ...), custom_call_target="tpu_custom_call" | custom-call | flops 1073741824 | bytes 1048576 | tf_op jit(solution)/shard_map/pallas_call | solution.py:445
  56.8 12.8 %all_to_all.20 = f32[32,2,128]{2,1,0:T(2,128)S(1)} all-to-all(f32[32,2,128]{2,1,0:T(2,128)S(1)} %bitcast.20), channel_id=1, replica_groups=mesh['state'=8,'plane'=16,'core'=2] {'plane','core'}, dimensions={0} | all-to-all | bytes 65536 | tf_op jit(solution)/shard_map/all_to_all | solution.py:452
  69.7 9.0 %all_to_all.21 = f32[8,2,128]{2,1,0:T(2,128)S(1)} all-to-all(f32[8,2,128]{2,1,0:T(2,128)S(1)} %broadcast_in_dim.2), channel_id=1, replica_groups=mesh['state'=8,'plane'=16,'core'=2] {'state'}, dimensions={0} | all-to-all | bytes 16384 | tf_op jit(solution)/shard_map/all_to_all | solution.py:454
  78.7 2.4 %shard_map.76 = f32[2304,128]{1,0:T(8,128)S(1)} custom-call(f32[16,128]{1,0:T(8,128)S(1)} %bitcast.19, f32[2,1024,128]{2,1,0:T(8,128)S(1)} %get-tuple-element.23.refs_1_, f32[1024,128]{1,0:T(8,128)S(1)} %get-tuple-element.24.refs_2_), custom_call_target="tpu_custom_call" | custom-call | flops 134217728 | bytes 1048576 | tf_op jit(solution)/shard_map/pallas_call | solution.py:456
  81.1 39.6 %all_to_all.22 = f32[256,1,1152]{2,1,0:T(1,128)S(1)} all-to-all(f32[256,1,1152]{2,1,0:T(1,128)S(1)} %bitcast.17), channel_id=1, replica_groups=mesh['state'=8,'plane'=16,'core'=2] {'state','core','plane'}, dimensions={0} | all-to-all | bytes 2359296 | tf_op jit(solution)/shard_map/all_to_all | solution.py:412
  120.8 2.1 %shard_map.77 = f32[2000,128]{1,0:T(8,128)} custom-call(f32[2304,128]{1,0:T(8,128)S(1)} %bitcast.16), custom_call_target="tpu_custom_call" | custom-call | flops 1048576 | bytes 1048576 | tf_op jit(solution)/shard_map/pallas_call | solution.py:464
  (2 shorter events, 0.1 us)
Async XLA Ops:
  3.8 15.7 %copy-start.4 = (f32[64,40]{0,1:T(8,128)S(1)}, f32[64,40]{0,1:T(8,128)}, u32[]{:S(2)}) copy-start(f32[64,40]{0,1:T(8,128)} %param.10) | copy-start | bytes 30724
  3.8 15.8 %copy-start = (f32[64,64]{1,0:T(8,128)S(1)}, f32[64,64]{1,0:T(8,128)}, u32[]{:S(2)}) copy-start(f32[64,64]{1,0:T(8,128)} %forward_ref.1) | copy-start | bytes 49156
  3.8 15.8 %copy-start.1 = (f32[64,64]{1,0:T(8,128)S(1)}, f32[64,64]{1,0:T(8,128)}, u32[]{:S(2)}) copy-start(f32[64,64]{1,0:T(8,128)} %back_ref.1) | copy-start | bytes 49156
  3.8 15.8 %copy-start.2 = (f32[40,40]{1,0:T(8,128)S(1)}, f32[40,40]{1,0:T(8,128)}, u32[]{:S(2)}) copy-start(f32[40,40]{1,0:T(8,128)} %mem_forward_ref.1) | copy-start | bytes 19204
  3.8 15.8 %copy-start.3 = (f32[40,40]{1,0:T(8,128)S(1)}, f32[40,40]{1,0:T(8,128)}, u32[]{:S(2)}) copy-start(f32[40,40]{1,0:T(8,128)} %mem_back_ref.1) | copy-start | bytes 19204
  3.8 48.6 %all-to-all-start = ((f32[256,1,1152]{2,1,0:T(1,128)}), f32[256,1,1152]{2,1,0:T(1,128)S(1)}, u32[]{:S(2)}, u32[]{:S(2)}) async-start(f32[256,1,1152]{2,1,0:T(1,128)} %bitcast.21), calls=%async_computation | async-start | bytes 2359296 | tf_op jit(solution)/shard_map/all_to_all | solution.py:412

commit v4 on v3

--- a/solution.py
+++ b/solution.py
@@ -76,9 +76,8 @@
 
             for v in range(13):
                 x_ref[e, 0:20, v * LANES : (v + 1) * LANES] = tile_in(v)
-                low = pltpu.roll(tile_in(12 + v), 64, 1)
-                high = pltpu.roll(tile_in(min(13 + v, 24)), 64, 1)
-                x_ref[e, 24:44, v * LANES : (v + 1) * LANES] = jnp.where(lane20 < 64, low, high)
+                odd = jnp.where(lane20 < 64, tile_in(min(13 + v, 24)), tile_in(12 + v))
+                x_ref[e, 24:44, v * LANES : (v + 1) * LANES] = turn(odd, 64)
             tile_ref[e] = dot3(step, split(x_ref[e]))
 
     def tile(e, v):
@@ -87,7 +86,7 @@
     def chunk(e, m):
         if m == 0:
             return tile(e, 0)
-        return jnp.where(lane < 8 * m, turn(tile(e, m - 1), 8 * m), turn(tile(e, m), 8 * m))
+        return turn(jnp.where(lane < LANES - 8 * m, tile(e, m), tile(e, m - 1)), 8 * m)
 
     copies = []
     for g in (6, 0, 1, 2, 3, 4, 5):
@@ -199,7 +198,7 @@
     size = GROUP * LEVELS
     groups = STATES // GROUP
 
-    lane = iota((32, LANES), 1)
+    lane = short = iota((32, LANES), 1)
     parts = []
     for part in range(2):
         sevenths = [recv_ref[pl.ds((2 * g + part) * 32 * ROWS + 8, 32, stride=ROWS), :] for g in range(groups)]
@@ -245,24 +244,27 @@
             rest_back = jnp.where(inside, turn(extra, 32 * group - at - 16), rest_back)
     rest = cavity(cb, rest_back)
     for group in range(groups):
-        rest_ref[group * size : (group + 1) * size, :] = jnp.where(lane < 24, turn(rest, -32 * group), 0.0)
+        for st in range(GROUP):
+            level = [rest[st * LEVELS + 32 * c : st * LEVELS + 32 * c + 32] for c in range(2)]
+            value = jnp.where(short < 24, turn(level[0], -32 * group), 0.0)
+            value = jnp.where((short >= 32) & (short < 56), turn(level[1], 32 - 32 * group), value)
+            at = (group * GROUP + st) * 32
+            rest_ref[at : at + 32, :] = value
 
     for first in range(0, STATES, 4):
         for second in range(0, first + 4, 4):
 
-            def add(tile, sums, first=first, second=second):
-                start = pl.multiple_of(tile * 8, 8)
-                for load in (
-                    lambda st: main_ref[0, pl.ds(st * LEVELS + start, 8), :],
-                    lambda st: main_ref[1, pl.ds(st * LEVELS + start, 8), :],
-                    lambda st: rest_ref[pl.ds(st * LEVELS + start, 8), :],
-                ):
-                    a = [load(first + n) for n in range(4)]
-                    b = a if first == second else [load(second + n) for n in range(4)]
-                    sums = tuple(sums[p * 4 + q] + a[p] * b[q] for p in range(4) for q in range(4))
-                return sums
-
-            sums = lax.fori_loop(0, 8, add, (jnp.zeros((8, LANES), F32),) * 16, unroll=True)
+            def add(tile, sums, load):
+                a = [load(first + n, tile) for n in range(4)]
+                b = a if first == second else [load(second + n, tile) for n in range(4)]
+                return tuple(sums[p * 4 + q] + a[p] * b[q] for p in range(4) for q in range(4))
+
+            sums = (jnp.zeros((8, LANES), F32),) * 16
+            for tile in range(8):
+                for h in range(2):
+                    sums = add(tile, sums, lambda st, n: main_ref[h, st * LEVELS + n * 8 : st * LEVELS + n * 8 + 8, :])
+            for tile in range(4):
+                sums = add(tile, sums, lambda st, n: rest_ref[st * 32 + n * 8 : st * 32 + n * 8 + 8, :])
             for p in range(4):
                 for q in range(4):
                     total = jnp.sum(sums[p * 4 + q], axis=0, keepdims=True)
@@ -290,10 +292,19 @@
     ]
     row, col = iota((STATES, LANES), 0), iota((STATES, LANES), 1)
     work = jnp.where(col < STATES, jnp.concatenate(square, axis=0), (col == row + STATES).astype(F32))
-    for j in range(STATES - 1):
-        pivot = work[j : j + 1, :]
-        pivot = pivot * (1.0 / jnp.broadcast_to(pivot[:, j : j + 1], (1, LANES)))
-        work = work - jnp.where(row > j, work[:, j : j + 1], 0.0) * pivot
+    def lanes(value, j):
+        return jnp.broadcast_to(value[:, j : j + 1], (value.shape[0], LANES))
+
+    for j in range(0, STATES, 2):
+        first, second = work[j : j + 1, :], work[j + 1 : j + 2, :]
+        left, right = lanes(work, j), lanes(work, j + 1)
+        side = lanes(first, j + 1)
+        over = 1.0 / lanes(first, j)
+        factor = side * over
+        below = 1.0 / (lanes(second, j + 1) - side * factor)
+        second = (second - factor * first) * below
+        right = right - left * factor
+        work = work - jnp.where(row > j, left, 0.0) * (first * over) - jnp.where(row > j + 1, right, 0.0) * second
     diagonal = jnp.sum(jnp.where(col == row, work, 0.0), axis=1, keepdims=True)
     inverse = work / jnp.sqrt(diagonal)
     for st in range(STATES):
@@ -305,10 +316,10 @@
     def mixed(loads):
         values = [[load(st) for load in loads] for st in range(STATES)]
         for t in range(STATES):
-            sums = [None, None]
+            sums = [None] * len(loads)
             for st in range(t + 1):
                 factor = coef_ref[st * STATES + t : st * STATES + t + 1, :]
-                for n in range(2):
+                for n in range(len(loads)):
                     term = factor * values[st][n]
                     sums[n] = term if sums[n] is None else sums[n] + term
             yield t, sums
@@ -324,15 +335,14 @@
                 for h in range(2):
                     at = (z * 32 + start) * ROWS + h * 4 + s * 2 + c
                     send_ref[pl.ds(at, 8, stride=ROWS), :] = sums[h]
-        loads = [lambda st, c=c: rest_ref[pl.ds(st * LEVELS + c * 32 + start, 8), :] for c in range(2)]
+        loads = [lambda st: rest_ref[pl.ds(st * 32 + start, 8), :]]
         seventh = None
         for t, sums in mixed(loads):
             z, s = t // 2, t % 2
-            for c in range(2):
-                e = s * 2 + c
-                value = pltpu.roll(sums[c], 32 * e, 1) if e else sums[c]
-                seventh = value if e == 0 else seventh + value
-            if s == 1:
+            if s == 0:
+                seventh = sums[0]
+            else:
+                seventh = seventh + turn(sums[0], 64)
                 send_ref[pl.ds((z * 32 + start) * ROWS + 8, 8, stride=ROWS), :] = seventh
         return carry
 
@@ -374,10 +384,10 @@
             for u in range(25):
                 if u < 12:
                     value = tile_ref[u, 0:20]
+                elif u == 12:
+                    value = jnp.where(lane20 < 64, tile_ref[12, 0:20], turn(tile_ref[0, 20:40], 64))
                 else:
-                    low = tile_ref[12, 0:20] if u == 12 else pltpu.roll(tile_ref[u - 13, 20:40], 64, 1)
-                    high = pltpu.roll(tile_ref[u - 12, 20:40], 64, 1)
-                    value = jnp.where(lane20 < 64, low, high)
+                    value = turn(jnp.where(lane20 < 64, tile_ref[u - 12, 20:40], tile_ref[u - 13, 20:40]), 64)
                 out_ref[pl.ds(s * 1000 + u * 2 + c, 20, stride=50), :] = value
         part = pl.ds(s * 1000, 1000)
         copies.append(pltpu.make_async_copy(out_ref.at[part], out_hbm.at[part], sems.at[s]))
@@ -425,7 +435,7 @@
         blocks,
         [
             pltpu.VMEM((256 * ROWS, LANES), F32),
-            pltpu.VMEM((2000, LANES), F32),
+            pltpu.VMEM((2208, LANES), F32),
             pltpu.VMEM((M, M), F32),
             pltpu.VMEM((4, 48, 13 * LANES), F32),
             pltpu.VMEM((4, M, 13 * LANES), F32),
@@ -444,7 +454,7 @@
     recv = exchange(send, everyone)
     main, rest, gram = call(
         step_kernel,
-        (shape(2, STATES * LEVELS, LANES), shape(STATES * LEVELS, LANES), shape(64, LANES)),
+        (shape(2, STATES * LEVELS, LANES), shape(STATES * 32, LANES), shape(64, LANES)),
         [pltpu.VMEM((STATES * STATES, LANES), F32)],
         1 << 30,
         "vvvvvvvv",
@@ -465,7 +475,7 @@
         tail_kernel,
         shape(2000, LANES),
         [
-            pltpu.VMEM((2000, LANES), F32),
+            pltpu.VMEM((2208, LANES), F32),
             pltpu.VMEM((4, 14, M, LANES), F32),
             pltpu.VMEM((4, 13, M, LANES), F32),
             pltpu.SemaphoreType.DMA((2,)),

time: 123 us -> 122 us (level)
  Pallas kernels: 14 us -> 12.7 us
where the time goes in v4:
time: 122 us
  blocking collectives  61.4 us (50%)
  waiting for transfers between devices  31.5 us (26%)
  starting transfers between devices  15.7 us (13%)
  Pallas kernels  12.7 us (10%)
    all_to_all x1, blocking collectives, exchange(): value = lax.all_to_all(value, axes, split_axis=0, concat_axis=0, tiled=True)  39.6 us
    all_to_all x1, waiting for transfers between devices, exchange(): value = lax.all_to_all(value, axes, split_axis=0, concat_axis=0, tiled=True)  31.5 us
    all_to_all x1, starting transfers between devices, exchange(): value = lax.all_to_all(value, axes, split_axis=0, concat_axis=0, tiled=True)  15.7 us
    all_to_all x1, blocking collectives, body(): lax.all_to_all(gram.reshape(32, 2, LANES), ('plane', 'core'), split_axis=...  12.8 us
    all_to_all x1, blocking collectives, body(): lax.all_to_all(gram, 'state', split_axis=0, concat_axis=0, tiled=True)  9.03 us
    pallas_call x1, Pallas kernels, body(): call(step_kernel, (shape(2, STATES * LEVELS, LANES), shape(STATES * 32, L...  3.88 us
    pallas_call x1, Pallas kernels, body(): call(head_kernel, blocks, [pltpu.VMEM((256 * ROWS, LANES), F32), pltpu.VM...  3.65 us
  transfers between devices with their start and end apart: 1, of which 1 were waited for; matrix products, arithmetic and copies ran while one was open for 0% of the time, Pallas kernels for 1%

profile of v4, /device:TPU:1, one launch (start us, length us, event | category | flops | bytes accessed | tf_op | source)
XLA Modules:
  0.0 121.6 jit_solution(11605668323504751289)
XLA Ops:
  0.0 3.6 %shard_map.73 = f32[2304,128]{1,0:T(8,128)} custom-call(f32[2000,128]{1,0:T(8,128)} %bitcast.22, f32[40,40]{1,0:T(8,128)} %step_hbm.1), custom_call_target="tpu_custom_call" | custom-call | flops 1048576 | bytes 1048576 | tf_op jit(solution)/shard_map/pallas_call | solution.py:433
  3.7 0.0 copy-start.4
  3.7 0.0 copy-start
  3.7 0.0 copy-start.1
  3.7 0.0 copy-start.2
  3.7 0.0 copy-start.3
  3.7 15.7 %all-to-all-start = ((f32[256,1,1152]{2,1,0:T(1,128)}), f32[256,1,1152]{2,1,0:T(1,128)S(1)}, u32[]{:S(2)}, u32[]{:S(2)}) async-start(f32[256,1,1152]{2,1,0:T(1,128)} %bitcast.21), calls=%async_computation | async-start | bytes 2359296 | tf_op jit(solution)/shard_map/all_to_all | solution.py:422
  19.4 0.0 copy-done.4
  19.4 0.1 copy.10.coupling_ref
  19.5 0.0 copy-done
  19.5 0.0 copy-done.1
  19.5 0.0 copy-done.2
  19.5 0.0 copy-done.3
  19.5 1.3 %shard_map.74 = (bf16[64,256]{1,0:T(8,128)(2,1)S(1)}, bf16[64,256]{1,0:T(8,128)(2,1)S(1)}, bf16[2,128,128]{2,1,0:T(8,128)(2,1)S(1)}, bf16[2,128,128]{2,1,0:T(8,1...) custom-call(f32[64,64]{1,0:T(8,128)S(1)} %copy-done, ...), custom_call_target="tpu_custom_call" | custom-call | flops 134217728 | bytes 1048576 | tf_op jit(solution)/shard_map/pallas_call | solution.py:451
  20.8 31.5 %all-to-all-done = f32[256,1,1152]{2,1,0:T(1,128)S(1)} async-done(((f32[256,1,1152]{2,1,0:T(1,128)}), f32[256,1,1152]{2,1,0:T(1,128)S(1)}, u32[]{:S(2)}, u32[]{:S(2)}) %all-to-all-start) | async-done | bytes 1179680 | tf_op jit(solution)/shard_map/all_to_all | solution.py:422
  52.3 3.9 %shard_map.75 = (f32[2,1024,128]{2,1,0:T(8,128)S(1)}, f32[512,128]{1,0:T(8,128)S(1)}, f32[64,128]{1,0:T(8,128)S(1)}) custom-call(f32[2304,128]{1,0:T(8,128)S(1)} %bitcast.18, bf16[64,256]{1,0:T(8,128)(2,1)S(1)} %get-tuple-element.15.cf_ref, bf16[64,256]{1,0:T(8,128)(2,1)S(1)} %get-tuple-element.16.cb_ref, bf16[2,128,128]{2,1,0:T(8,128)(2,1)S(1)} %get-tuple-element.17.mf_ref, ...), custom_call_target="tpu_custom_call" | custom-call | flops 1073741824 | bytes 1048576 | tf_op jit(solution)/shard_map/pallas_call | solution.py:455
  56.2 12.8 %all_to_all.20 = f32[32,2,128]{2,1,0:T(2,128)S(1)} all-to-all(f32[32,2,128]{2,1,0:T(2,128)S(1)} %bitcast.20), channel_id=1, replica_groups=mesh['state'=8,'plane'=16,'core'=2] {'plane','core'}, dimensions={0} | all-to-all | bytes 65536 | tf_op jit(solution)/shard_map/all_to_all | solution.py:462
  69.0 9.0 %all_to_all.21 = f32[8,2,128]{2,1,0:T(2,128)S(1)} all-to-all(f32[8,2,128]{2,1,0:T(2,128)S(1)} %broadcast_in_dim.2), channel_id=1, replica_groups=mesh['state'=8,'plane'=16,'core'=2] {'state'}, dimensions={0} | all-to-all | bytes 16384 | tf_op jit(solution)/shard_map/all_to_all | solution.py:464
  78.1 1.8 %shard_map.76 = f32[2304,128]{1,0:T(8,128)S(1)} custom-call(f32[16,128]{1,0:T(8,128)S(1)} %bitcast.19, f32[2,1024,128]{2,1,0:T(8,128)S(1)} %get-tuple-element.23.refs_1_, f32[512,128]{1,0:T(8,128)S(1)} %get-tuple-element.24.refs_2_), custom_call_target="tpu_custom_call" | custom-call | flops 134217728 | bytes 1048576 | tf_op jit(solution)/shard_map/pallas_call | solution.py:466
  79.8 39.6 %all_to_all.22 = f32[256,1,1152]{2,1,0:T(1,128)S(1)} all-to-all(f32[256,1,1152]{2,1,0:T(1,128)S(1)} %bitcast.16), channel_id=1, replica_groups=mesh['state'=8,'plane'=16,'core'=2] {'state','core','plane'}, dimensions={0} | all-to-all | bytes 2359296 | tf_op jit(solution)/shard_map/all_to_all | solution.py:422
  119.5 2.1 %shard_map.77 = f32[2000,128]{1,0:T(8,128)} custom-call(f32[2304,128]{1,0:T(8,128)S(1)} %bitcast.17), custom_call_target="tpu_custom_call" | custom-call | flops 1048576 | bytes 1048576 | tf_op jit(solution)/shard_map/pallas_call | solution.py:474
  (2 shorter events, 0.1 us)
Async XLA Ops:
  3.7 15.7 %copy-start.4 = (f32[64,40]{0,1:T(8,128)S(1)}, f32[64,40]{0,1:T(8,128)}, u32[]{:S(2)}) copy-start(f32[64,40]{0,1:T(8,128)} %param.10) | copy-start | bytes 30724
  3.7 15.8 %copy-start = (f32[64,64]{1,0:T(8,128)S(1)}, f32[64,64]{1,0:T(8,128)}, u32[]{:S(2)}) copy-start(f32[64,64]{1,0:T(8,128)} %forward_ref.1) | copy-start | bytes 49156
  3.7 15.8 %copy-start.1 = (f32[64,64]{1,0:T(8,128)S(1)}, f32[64,64]{1,0:T(8,128)}, u32[]{:S(2)}) copy-start(f32[64,64]{1,0:T(8,128)} %back_ref.1) | copy-start | bytes 49156
  3.7 15.8 %copy-start.2 = (f32[40,40]{1,0:T(8,128)S(1)}, f32[40,40]{1,0:T(8,128)}, u32[]{:S(2)}) copy-start(f32[40,40]{1,0:T(8,128)} %mem_forward_ref.1) | copy-start | bytes 19204
  3.7 15.8 %copy-start.3 = (f32[40,40]{1,0:T(8,128)S(1)}, f32[40,40]{1,0:T(8,128)}, u32[]{:S(2)}) copy-start(f32[40,40]{1,0:T(8,128)} %mem_back_ref.1) | copy-start | bytes 19204
  3.7 48.6 %all-to-all-start = ((f32[256,1,1152]{2,1,0:T(1,128)}), f32[256,1,1152]{2,1,0:T(1,128)S(1)}, u32[]{:S(2)}, u32[]{:S(2)}) async-start(f32[256,1,1152]{2,1,0:T(1,128)} %bitcast.21), calls=%async_computation | async-start | bytes 2359296 | tf_op jit(solution)/shard_map/all_to_all | solution.py:422

commit v5 on v4

--- a/solution.py
+++ b/solution.py
@@ -54,7 +54,7 @@
         copies[-1].start()
     for e in range(4):
         for row in (16, 40):
-            x_ref[e, row : row + 8, :] = jnp.zeros((8, 13 * LANES), F32)
+            x_ref[e, row : row + 8, :] = jnp.zeros((8, 14 * LANES), F32)
     send_ref[pl.ds(80 * ROWS + 8, 176, stride=ROWS), :] = jnp.zeros((176, LANES), F32)
     row, col = iota((M, M), 0), iota((M, M), 1)
     order = (col == jnp.where(row < 20, 2 * row, 2 * row - 39)).astype(F32)
@@ -74,19 +74,19 @@
             def tile_in(u):
                 return states_ref[pl.ds(s * 1000 + u * 2 + c, 20, stride=50), :]
 
-            for v in range(13):
-                x_ref[e, 0:20, v * LANES : (v + 1) * LANES] = tile_in(v)
-                odd = jnp.where(lane20 < 64, tile_in(min(13 + v, 24)), tile_in(12 + v))
-                x_ref[e, 24:44, v * LANES : (v + 1) * LANES] = turn(odd, 64)
+            for m in range(14):
+                at = slice(m * LANES, (m + 1) * LANES)
+                value = tile_in(0)
+                if m:
+                    value = turn(jnp.where(lane20 < LANES - 8 * m, tile_in(m), tile_in(m - 1)), 8 * m)
+                x_ref[e, 0:20, at] = value
+                first, offset = divmod(1600 + 120 * m, LANES)
+                value = jnp.where(lane20 >= offset, tile_in(first), tile_in(min(first + 1, 24)))
+                x_ref[e, 24:44, at] = turn(value, -offset)
             tile_ref[e] = dot3(step, split(x_ref[e]))
 
-    def tile(e, v):
-        return tile_ref[e, :, v * LANES : (v + 1) * LANES]
-
     def chunk(e, m):
-        if m == 0:
-            return tile(e, 0)
-        return turn(jnp.where(lane < LANES - 8 * m, tile(e, m), tile(e, m - 1)), 8 * m)
+        return tile_ref[e, :, m * LANES : (m + 1) * LANES]
 
     copies = []
     for g in (6, 0, 1, 2, 3, 4, 5):
@@ -99,7 +99,7 @@
                     send_ref[pl.ds(240 * ROWS + h * 4 + e, 16, stride=ROWS), :] = block
                 continue
             if g == 0:
-                seventh = turn(tile(e, 12), -24)
+                seventh = chunk(e, 13)
             elif g == 1:
                 tail = chunk(e, 12)[32:40]
                 tails = [tail, turn(tail, -40), turn(tail, -80), jnp.zeros((16, LANES), F32)]
@@ -437,8 +437,8 @@
             pltpu.VMEM((256 * ROWS, LANES), F32),
             pltpu.VMEM((2208, LANES), F32),
             pltpu.VMEM((M, M), F32),
-            pltpu.VMEM((4, 48, 13 * LANES), F32),
-            pltpu.VMEM((4, M, 13 * LANES), F32),
+            pltpu.VMEM((4, 48, 14 * LANES), F32),
+            pltpu.VMEM((4, M, 14 * LANES), F32),
             pltpu.SemaphoreType.DMA((10,)),
         ],
         1 << 20,

time: 122 us -> 122 us (level)
  no operation moved by 1% of the time
where the time goes in v5:
time: 122 us; the launch traced here: 121 us
  blocking collectives  61.4 us (50%)
  waiting for transfers between devices  31.5 us (26%)
  starting transfers between devices  15.7 us (13%)
  Pallas kernels  12.5 us (10%)
    all_to_all x1, blocking collectives, exchange(): value = lax.all_to_all(value, axes, split_axis=0, concat_axis=0, tiled=True)  39.6 us
    all_to_all x1, waiting for transfers between devices, exchange(): value = lax.all_to_all(value, axes, split_axis=0, concat_axis=0, tiled=True)  31.5 us
    all_to_all x1, starting transfers between devices, exchange(): value = lax.all_to_all(value, axes, split_axis=0, concat_axis=0, tiled=True)  15.7 us
    all_to_all x1, blocking collectives, body(): lax.all_to_all(gram.reshape(32, 2, LANES), ('plane', 'core'), split_axis=...  12.8 us
    all_to_all x1, blocking collectives, body(): lax.all_to_all(gram, 'state', split_axis=0, concat_axis=0, tiled=True)  9.03 us
    pallas_call x1, Pallas kernels, body(): call(step_kernel, (shape(2, STATES * LEVELS, LANES), shape(STATES * 32, L...  3.89 us
    pallas_call x1, Pallas kernels, body(): call(head_kernel, blocks, [pltpu.VMEM((256 * ROWS, LANES), F32), pltpu.VM...  3.5 us
  transfers between devices with their start and end apart: 1, of which 1 were waited for; matrix products, arithmetic and copies ran while one was open for 0% of the time, Pallas kernels for 1%

profile of v5, /device:TPU:1, one launch (start us, length us, event | category | flops | bytes accessed | tf_op | source)
XLA Modules:
  0.0 121.4 jit_solution(16756643583628465956)
XLA Ops:
  0.0 3.5 %shard_map.73 = f32[2304,128]{1,0:T(8,128)} custom-call(f32[2000,128]{1,0:T(8,128)} %bitcast.22, f32[40,40]{1,0:T(8,128)} %step_hbm.1), custom_call_target="tpu_custom_call" | custom-call | flops 1048576 | bytes 1048576 | tf_op jit(solution)/shard_map/pallas_call | solution.py:433
  3.5 0.0 copy-start.4
  3.5 0.0 copy-start
  3.5 0.0 copy-start.1
  3.5 0.0 copy-start.2
  3.6 0.0 copy-start.3
  3.6 15.7 %all-to-all-start = ((f32[256,1,1152]{2,1,0:T(1,128)}), f32[256,1,1152]{2,1,0:T(1,128)S(1)}, u32[]{:S(2)}, u32[]{:S(2)}) async-start(f32[256,1,1152]{2,1,0:T(1,128)} %bitcast.21), calls=%async_computation | async-start | bytes 2359296 | tf_op jit(solution)/shard_map/all_to_all | solution.py:422
  19.2 0.0 copy-done.4
  19.3 0.1 copy.10.coupling_ref
  19.3 0.0 copy-done
  19.3 0.0 copy-done.1
  19.3 0.0 copy-done.2
  19.4 0.0 copy-done.3
  19.4 1.3 %shard_map.74 = (bf16[64,256]{1,0:T(8,128)(2,1)S(1)}, bf16[64,256]{1,0:T(8,128)(2,1)S(1)}, bf16[2,128,128]{2,1,0:T(8,128)(2,1)S(1)}, bf16[2,128,128]{2,1,0:T(8,1...) custom-call(f32[64,64]{1,0:T(8,128)S(1)} %copy-done, ...), custom_call_target="tpu_custom_call" | custom-call | flops 134217728 | bytes 1048576 | tf_op jit(solution)/shard_map/pallas_call | solution.py:451
  20.6 31.5 %all-to-all-done = f32[256,1,1152]{2,1,0:T(1,128)S(1)} async-done(((f32[256,1,1152]{2,1,0:T(1,128)}), f32[256,1,1152]{2,1,0:T(1,128)S(1)}, u32[]{:S(2)}, u32[]{:S(2)}) %all-to-all-start) | async-done | bytes 1179680 | tf_op jit(solution)/shard_map/all_to_all | solution.py:422
  52.2 3.9 %shard_map.75 = (f32[2,1024,128]{2,1,0:T(8,128)S(1)}, f32[512,128]{1,0:T(8,128)S(1)}, f32[64,128]{1,0:T(8,128)S(1)}) custom-call(f32[2304,128]{1,0:T(8,128)S(1)} %bitcast.18, bf16[64,256]{1,0:T(8,128)(2,1)S(1)} %get-tuple-element.15.cf_ref, bf16[64,256]{1,0:T(8,128)(2,1)S(1)} %get-tuple-element.16.cb_ref, bf16[2,128,128]{2,1,0:T(8,128)(2,1)S(1)} %get-tuple-element.17.mf_ref, ...), custom_call_target="tpu_custom_call" | custom-call | flops 1073741824 | bytes 1048576 | tf_op jit(solution)/shard_map/pallas_call | solution.py:455
  56.1 12.8 %all_to_all.20 = f32[32,2,128]{2,1,0:T(2,128)S(1)} all-to-all(f32[32,2,128]{2,1,0:T(2,128)S(1)} %bitcast.20), channel_id=1, replica_groups=mesh['state'=8,'plane'=16,'core'=2] {'plane','core'}, dimensions={0} | all-to-all | bytes 65536 | tf_op jit(solution)/shard_map/all_to_all | solution.py:462
  68.9 9.0 %all_to_all.21 = f32[8,2,128]{2,1,0:T(2,128)S(1)} all-to-all(f32[8,2,128]{2,1,0:T(2,128)S(1)} %broadcast_in_dim.2), channel_id=1, replica_groups=mesh['state'=8,'plane'=16,'core'=2] {'state'}, dimensions={0} | all-to-all | bytes 16384 | tf_op jit(solution)/shard_map/all_to_all | solution.py:464
  77.9 1.8 %shard_map.76 = f32[2304,128]{1,0:T(8,128)S(1)} custom-call(f32[16,128]{1,0:T(8,128)S(1)} %bitcast.19, f32[2,1024,128]{2,1,0:T(8,128)S(1)} %get-tuple-element.23.refs_1_, f32[512,128]{1,0:T(8,128)S(1)} %get-tuple-element.24.refs_2_), custom_call_target="tpu_custom_call" | custom-call | flops 134217728 | bytes 1048576 | tf_op jit(solution)/shard_map/pallas_call | solution.py:466
  79.7 39.6 %all_to_all.22 = f32[256,1,1152]{2,1,0:T(1,128)S(1)} all-to-all(f32[256,1,1152]{2,1,0:T(1,128)S(1)} %bitcast.16), channel_id=1, replica_groups=mesh['state'=8,'plane'=16,'core'=2] {'state','core','plane'}, dimensions={0} | all-to-all | bytes 2359296 | tf_op jit(solution)/shard_map/all_to_all | solution.py:422
  119.3 2.1 %shard_map.77 = f32[2000,128]{1,0:T(8,128)} custom-call(f32[2304,128]{1,0:T(8,128)S(1)} %bitcast.17), custom_call_target="tpu_custom_call" | custom-call | flops 1048576 | bytes 1048576 | tf_op jit(solution)/shard_map/pallas_call | solution.py:474
  (2 shorter events, 0.1 us)
Async XLA Ops:
  3.5 15.7 %copy-start.4 = (f32[64,40]{0,1:T(8,128)S(1)}, f32[64,40]{0,1:T(8,128)}, u32[]{:S(2)}) copy-start(f32[64,40]{0,1:T(8,128)} %param.10) | copy-start | bytes 30724
  3.5 15.8 %copy-start = (f32[64,64]{1,0:T(8,128)S(1)}, f32[64,64]{1,0:T(8,128)}, u32[]{:S(2)}) copy-start(f32[64,64]{1,0:T(8,128)} %forward_ref.1) | copy-start | bytes 49156
  3.5 15.8 %copy-start.1 = (f32[64,64]{1,0:T(8,128)S(1)}, f32[64,64]{1,0:T(8,128)}, u32[]{:S(2)}) copy-start(f32[64,64]{1,0:T(8,128)} %back_ref.1) | copy-start | bytes 49156
  3.5 15.8 %copy-start.2 = (f32[40,40]{1,0:T(8,128)S(1)}, f32[40,40]{1,0:T(8,128)}, u32[]{:S(2)}) copy-start(f32[40,40]{1,0:T(8,128)} %mem_forward_ref.1) | copy-start | bytes 19204
  3.6 15.8 %copy-start.3 = (f32[40,40]{1,0:T(8,128)S(1)}, f32[40,40]{1,0:T(8,128)}, u32[]{:S(2)}) copy-start(f32[40,40]{1,0:T(8,128)} %mem_back_ref.1) | copy-start | bytes 19204
  3.6 48.6 %all-to-all-start = ((f32[256,1,1152]{2,1,0:T(1,128)}), f32[256,1,1152]{2,1,0:T(1,128)S(1)}, u32[]{:S(2)}, u32[]{:S(2)}) async-start(f32[256,1,1152]{2,1,0:T(1,128)} %bitcast.21), calls=%async_computation | async-start | bytes 2359296 | tf_op jit(solution)/shard_map/all_to_all | solution.py:422
